TPU v7x, 32 devices: a whole 2x2x4 slice. The times are simulated.
32 devices in a mesh: grp: 2 (over x), brick: 8 (over z, y), cuts: 2 (over core).
Axes of the slice: x: 2, y: 2, z: 4, core: 2. Of those that a mesh axis runs over, the one named last changes fastest.
Arguments:
- initial: float32 [3, 512, 5120], P(None, ('grp', 'brick')), parts along dimension 1, may hold values from -3 to 3
- depth: float32 [256, 5120], P('brick'), may hold values from 0.5 to 2.5
- mask: int32 [256, 5120], P('brick'), may hold values 0 or 1
Outputs:
- ends: float32 [2, 3, 512, 5120], P('cuts', None, ('grp', 'brick')), parts along dimension 2
There are 2 independent parts, one for each index of `grp`. A program takes and returns all parts, laid end to end along the dimension named above; an argument that names none is the same for every part. Nothing has to cross between parts.
Inputs may be any that keep to these rules, and one draw needn't show every extreme that they name: `mask`: 1 marks an ocean cell, 0 land.
All inputs are finite; a program needn't handle non-finite values. No bound on the sum of `mask` on one device may be relied on, other than what follows from the above.
Results may differ from a plain program's by a relative error of at most 0.0001.
Values sent between devices are 32-bit elements; how exact they have to be, the bound alone decides.
No kernel may reach another device: no remote copies, remote signals or barrier semaphores. Data moves between devices by JAX's collectives and lax.ppermute only.
A program may use at most 64 MiB of HBM per device.

v0:
```python
import functools

import jax
import jax.numpy as jnp
from jax import lax
from jax.experimental import pallas as pl
from jax.experimental.pallas import tpu as pltpu
from jax.sharding import PartitionSpec as P


COURANT = 0.2
DIFFUSION = 0.05
FRICTION = 0.01
CORIOLIS = 0.5
FINE_TIME = 0.2
COARSE_TIME = 0.4
SUB, LANES = 8, 128
HALO = 4
PER = 5
PACKED = HALO * PER - 1
VMEM_LIMIT = 40 * 1024 * 1024


def next_col(x, amount, edge):
    turned = [pltpu.roll(a, LANES - amount, 1) for a in x]
    turned.append(pltpu.roll(turned[0], SUB - 1, 0))
    return [jnp.where(edge, turned[j + 1], turned[j]) for j in range(len(x))]


def prev_col(x, amount, edge):
    turned = [pltpu.roll(a, amount, 1) for a in x]
    turned.insert(0, pltpu.roll(turned[-1], 1, 0))
    return [jnp.where(edge, turned[j], turned[j + 1]) for j in range(len(x))]


def lane_ids():
    return lax.broadcasted_iota(jnp.int32, (SUB, LANES), 1)


def step(state, depth, wet, turn, dt, cols):
    (eb, ub, vb), (e, u, v), (ea, ua, va) = state
    hb, h, ha = depth
    lane = lane_ids()
    last, first = lane >= LANES - cols, lane < cols
    nj = len(e)
    g = [(h[j] + e[j]) * v[j] for j in range(nj)]
    e_r, e_l = next_col(e, cols, last), prev_col(e, cols, first)
    u_r, u_l = next_col(u, cols, last), prev_col(u, cols, first)
    v_r, v_l = next_col(v, cols, last), prev_col(v, cols, first)
    g_r, g_l = next_col(g, cols, last), prev_col(g, cols, first)
    half = 0.5 * COURANT
    keep_e = 1.0 - 4.0 * DIFFUSION
    keep = 1.0 - dt * FRICTION - 4.0 * DIFFUSION
    new_e, new_u, new_v = [], [], []
    for j in range(nj):
        flux = ((ha[j] + ea[j]) * ua[j] - (hb[j] + eb[j]) * ub[j]) + (g_r[j] - g_l[j])
        around = (ea[j] + eb[j]) + (e_r[j] + e_l[j])
        new_e.append(keep_e * e[j] + (DIFFUSION * around - half * flux))
        a, b = half * u[j], half * v[j]
        a_up, a_dn, b_up, b_dn = DIFFUSION - a, DIFFUSION + a, DIFFUSION - b, DIFFUSION + b
        nu = (keep * u[j] + turn * v[j]) - half * (ea[j] - eb[j])
        nu = nu + ((ua[j] * a_up + ub[j] * a_dn) + (u_r[j] * b_up + u_l[j] * b_dn))
        nv = (keep * v[j] - turn * u[j]) - half * (e_r[j] - e_l[j])
        nv = nv + ((va[j] * a_up + vb[j] * a_dn) + (v_r[j] * b_up + v_l[j] * b_dn))
        new_u.append(nu * wet[j])
        new_v.append(nv * wet[j])
    return new_e, new_u, new_v


def average(low, high):
    even = lane_ids() % 2 == 0
    out = []
    for a, b in zip(low, high):
        s = a + b
        out.append((s + jnp.where(even, pltpu.roll(s, LANES - 1, 1), pltpu.roll(s, 1, 1))) * 0.25)
    return out


def rows_of(ref, *at):
    return [ref[(*at, j)] for j in range(ref.shape[-3])]


def put(ref, at, row):
    for j, a in enumerate(row):
        ref[(*at, j)] = a


def three(ref, at):
    return tuple(rows_of(ref, at, k) for k in range(3))


def put_three(ref, at, rows):
    for k, row in enumerate(rows):
        put(ref, (at, k), row)


def scaled(rows, factor):
    e, u, v = rows
    return [a * factor for a in e], u, v


def turning(row, first_row, scale, all_rows, dt):
    y = (first_row + row).astype(jnp.float32) * (2.0 * scale) + scale
    return (dt * CORIOLIS) * (y * (1.0 / all_rows) - 1.0)


def tile_row(nj, row, j):
    wide = nj * SUB
    return pl.ds((row // SUB) * (wide * SUB) + row % SUB + j * SUB, SUB, stride=nj * SUB)


def pack_kernel(nj, initial, depth, mask, out, initial_v, depth_v, mask_v, sems):
    lane = lax.axis_index("cuts")
    tile = nj * SUB * SUB
    high = initial.shape[1] // tile - 1
    start = pl.multiple_of(jnp.where(lane == 0, high, 0) * tile, tile)
    copies = [
        pltpu.make_async_copy(initial.at[:, pl.ds(start, tile), :], initial_v, sems.at[0]),
        pltpu.make_async_copy(depth.at[pl.ds(start, tile), :], depth_v, sems.at[1]),
        pltpu.make_async_copy(mask.at[pl.ds(start, tile), :], mask_v, sems.at[2]),
    ]
    for copy in copies:
        copy.start()
    for copy in copies:
        copy.wait()

    def fill(row_of):
        for d in range(HALO):
            for j in range(nj):
                at = tile_row(nj, row_of(d), j)
                for k in range(3):
                    out[d * PER + k, j] = initial_v[k, at, :]
                out[d * PER + 3, j] = depth_v[at, :]
                if d < HALO - 1:
                    out[d * PER + 4, j] = mask_v[at, :].astype(jnp.float32)

    pl.when(lane == 0)(lambda: fill(lambda d: SUB - 1 - d))
    pl.when(lane != 0)(lambda: fill(lambda d: d))


MID_INIT, MID_DEPTH, MID_WET, MID_ONE, MID_RF, MID_C1, MID_PONE = 0, 12, 18, 22, 28, 34, 40
MID = 46


def middle_kernel(nj, bricks, initial, depth, mask, out, mid, ini, hw, s1, s2, rc, rhw, c1, p1, dif):
    lane = lax.axis_index("cuts")
    brick = lax.axis_index("brick")
    n = ini.shape[0]
    m = n // 2
    all_rows = n * bricks

    def own(side, i, count=n):
        return i if side == 0 else count - 1 - i

    def load(t, carry):
        for r in range(SUB):
            row = t * SUB + r
            for j in range(nj):
                at = pl.ds(t * (nj * SUB * SUB) + r + j * SUB, SUB, stride=nj * SUB)
                for k in range(3):
                    ini[row, k, j] = initial[k, at, :]
                hw[row, 0, j] = depth[at, :]
                hw[row, 1, j] = mask[at, :].astype(jnp.float32)
        return carry

    lax.fori_loop(0, n // SUB, load, 0)

    def h3(row):
        return tuple(rows_of(hw, row + d, 0) for d in (-1, 0, 1))

    def fine(src, dst):
        def body(row, carry):
            state = tuple(three(src, row + d) for d in (-1, 0, 1))
            turn = turning(row, brick * n, 1.0, all_rows, FINE_TIME)
            put_three(dst, row, step(state, h3(row), rows_of(hw, row, 1), turn, FINE_TIME, 1))
            return carry

        return body

    lax.fori_loop(1, n - 1, fine(ini, s1), 0)
    lax.fori_loop(2, n - 2, fine(s1, s2), 0)

    for side in (0, 1):
        for i in range(4):
            put_three_mid(mid, side, MID_INIT + 3 * i, three(ini, own(side, i)))
            put(mid, (side, MID_WET + i), rows_of(hw, own(side, i), 1))
        for i in range(6):
            put(mid, (side, MID_DEPTH + i), rows_of(hw, own(side, i), 0))
        for i in (1, 2):
            put_three_mid(mid, side, MID_ONE + 3 * (i - 1), three(s1, own(side, i)))

    def emit(row, rows):
        for k in range(3):
            for j in range(nj):
                at = pl.ds((row // SUB) * (nj * SUB * SUB) + row % SUB + j * SUB, SUB, stride=nj * SUB)
                out[k, at, :] = rows[k][j]

    @pl.when(lane == 0)
    def _():
        def body(row, carry):
            emit(row, three(s2, row))
            return carry

        lax.fori_loop(2, n - 2, body, 0)

    @pl.when(lane != 0)
    def _():
        def restrict(row, carry):
            lo, hi = three(ini, 2 * row), three(ini, 2 * row + 1)
            put_three(rc, row, [average(a, b) for a, b in zip(lo, hi)])
            for k in range(2):
                put(rhw, (row, k), average(rows_of(hw, 2 * row, k), rows_of(hw, 2 * row + 1, k)))
            return carry

        lax.fori_loop(0, m, restrict, 0)

        def coarse(src, row):
            state = tuple(three(src, row + d) for d in (-1, 0, 1))
            heights = tuple(rows_of(rhw, row + d, 0) for d in (-1, 0, 1))
            turn = turning(row, brick * m, 2.0, all_rows, COARSE_TIME)
            return step(state, heights, rows_of(rhw, row, 1), turn, COARSE_TIME, 2)

        def first(row, carry):
            put_three(c1, row, coarse(rc, row))
            return carry

        lax.fori_loop(1, m - 1, first, 0)

        def again(row, carry):
            lo, hi = three(s2, 2 * row), three(s2, 2 * row + 1)
            put_three(rc, row, [average(a, b) for a, b in zip(lo, hi)])
            return carry

        lax.fori_loop(1, m - 1, again, 0)
        for side in (0, 1):
            for i in (1, 2):
                put_three_mid(mid, side, MID_RF + 3 * (i - 1), three(rc, own(side, i, m)))
                put_three_mid(mid, side, MID_C1 + 3 * (i - 1), three(c1, own(side, i, m)))

        def correct(row, carry):
            fresh, old = coarse(rc, row), coarse(c1, row)
            put_three(dif, row, [[a - b for a, b in zip(x, y)] for x, y in zip(fresh, old)])
            return carry

        lax.fori_loop(2, m - 2, correct, 0)

        def prolonged(row, carry):
            state = tuple(three(c1, (row + d) // 2) for d in (-1, 0, 1))
            turn = turning(row, brick * n, 1.0, all_rows, FINE_TIME)
            put_three(p1, row, step(state, h3(row), rows_of(hw, row, 1), turn, FINE_TIME, 1))
            return carry

        lax.fori_loop(3, n - 3, prolonged, 0)
        for side in (0, 1):
            for i in (3, 4):
                put_three_mid(mid, side, MID_PONE + 3 * (i - 3), three(p1, own(side, i)))

        def last(row, carry):
            state = tuple(three(p1, row + d) for d in (-1, 0, 1))
            turn = turning(row, brick * n, 1.0, all_rows, FINE_TIME)
            rows = step(state, h3(row), rows_of(hw, row, 1), turn, FINE_TIME, 1)
            add = three(dif, row // 2)
            emit(row, [[a + b for a, b in zip(x, y)] for x, y in zip(rows, add)])
            return carry

        lax.fori_loop(4, n - 4, last, 0)


def put_three_mid(mid, side, at, rows):
    for k, row in enumerate(rows):
        put(mid, (side, at + k), row)


def edge_kernel(nj, bricks, n, low1, high1, low0, high0, mid, before, out, halo, midv, tiles, sems):
    lane = lax.axis_index("cuts")
    brick = lax.axis_index("brick")
    all_rows = n * bricks
    m = n // 2
    tile = nj * SUB * SUB
    high_tile = (n // SUB - 1) * tile
    spots = (0, high_tile)
    fetch = [pltpu.make_async_copy(mid.at[s], midv.at[s], sems.at[s]) for s in (0, 1)]
    fetch += [
        pltpu.make_async_copy(before.at[:, pl.ds(spots[s], tile), :], tiles.at[s], sems.at[2 + s])
        for s in (0, 1)
    ]
    for copy in fetch:
        copy.start()

    def halos(low, high):
        got = [pltpu.make_async_copy(a, halo.at[s], sems.at[4 + s]) for s, a in enumerate((low, high))]
        for copy in got:
            copy.start()
        for copy in got:
            copy.wait()

    pl.when(lane == 0)(lambda: halos(low0, high0))
    pl.when(lane != 0)(lambda: halos(low1, high1))
    for copy in fetch:
        copy.wait()

    def initial(s, i):
        if i < 0:
            return tuple(rows_of(halo, s, (-1 - i) * PER + k) for k in range(3))
        return tuple(rows_of(midv, s, MID_INIT + 3 * i + k) for k in range(3))

    def depth(s, i):
        return rows_of(halo, s, (-1 - i) * PER + 3) if i < 0 else rows_of(midv, s, MID_DEPTH + i)

    def wet(s, i):
        return rows_of(halo, s, (-1 - i) * PER + 4) if i < 0 else rows_of(midv, s, MID_WET + i)

    def kept(s, base):
        return tuple(rows_of(midv, s, base + k) for k in range(3))

    def inside(s):
        there = brick > 0 if s == 0 else brick < bricks - 1
        return jnp.where(there, 1.0, 0.0).astype(jnp.float32)

    def order(s, f):
        return (f(-1), f(0), f(1)) if s == 0 else (f(1), f(0), f(-1))

    def fine(s, i, state, real):
        row = jnp.int32(i if s == 0 else n - 1 - i)
        turn = turning(row, brick * n, 1.0, all_rows, FINE_TIME)
        new = step(order(s, lambda d: state(i + d)), order(s, lambda d: depth(s, i + d)), wet(s, i), turn, FINE_TIME, 1)
        return scaled(new, real) if i < 0 else new

    def coarse(s, i, state, depths, wets, real):
        row = jnp.int32(i if s == 0 else m - 1 - i)
        turn = turning(row, brick * m, 2.0, all_rows, COARSE_TIME)
        new = step(order(s, lambda d: state(i + d)), order(s, lambda d: depths(i + d)), wets(i), turn, COARSE_TIME, 2)
        return scaled(new, real) if i < 0 else new

    def both(a, b):
        return tuple(average(x, y) for x, y in zip(a, b))

    def emit(s, i, rows):
        r = i if s == 0 else SUB - 1 - i
        for k in range(3):
            for j in range(nj):
                tiles[s, k, pl.ds(r + j * SUB, SUB, stride=nj * SUB), :] = rows[k][j]

    def flown(s, outer, real):
        one = {i: fine(s, i, lambda i: initial(s, i), real) for i in range(outer - 1, 1)}
        one.update({i: kept(s, MID_ONE + 3 * (i - 1)) for i in (1, 2)})
        return {i: fine(s, i, one.__getitem__, real) for i in range(outer, 2)}

    @pl.when(lane == 0)
    def _():
        for s in (0, 1):
            two = flown(s, 0, inside(s))
            for i in (0, 1):
                emit(s, i, two[i])

    @pl.when(lane != 0)
    def _():
        for s in (0, 1):
            real = inside(s)
            two = flown(s, -2, real)
            fresh = {i: both(two[2 * i], two[2 * i + 1]) for i in (-1, 0)}
            fresh.update({i: kept(s, MID_RF + 3 * (i - 1)) for i in (1, 2)})
            start = {i: both(initial(s, 2 * i), initial(s, 2 * i + 1)) for i in (-2, -1, 0, 1)}
            deep = {i: average(depth(s, 2 * i), depth(s, 2 * i + 1)) for i in range(-2, 3)}
            dry = {i: average(wet(s, 2 * i), wet(s, 2 * i + 1)) for i in (-1, 0, 1)}
            c1 = {i: coarse(s, i, start.__getitem__, deep.__getitem__, dry.__getitem__, real) for i in (-1, 0)}
            c1.update({i: kept(s, MID_C1 + 3 * (i - 1)) for i in (1, 2)})
            add = {}
            for i in (0, 1):
                x = coarse(s, i, fresh.__getitem__, deep.__getitem__, dry.__getitem__, real)
                y = coarse(s, i, c1.__getitem__, deep.__getitem__, dry.__getitem__, real)
                add[i] = [[a - b for a, b in zip(p, q)] for p, q in zip(x, y)]
            one = {i: fine(s, i, lambda i: c1[i // 2], real) for i in range(-1, 3)}
            one.update({i: kept(s, MID_PONE + 3 * (i - 3)) for i in (3, 4)})
            for i in range(4):
                rows = fine(s, i, one.__getitem__, real)
                emit(s, i, [[a + b for a, b in zip(x, y)] for x, y in zip(rows, add[i // 2])])

    back = [
        pltpu.make_async_copy(tiles.at[s], out.at[:, pl.ds(spots[s], tile), :], sems.at[2 + s])
        for s in (0, 1)
    ]
    for copy in back:
        copy.start()
    for copy in back:
        copy.wait()


def tiled(a):
    *lead, rows, cols = a.shape
    a = a.reshape(*lead, rows // SUB, SUB, cols // LANES, LANES)
    return jnp.swapaxes(a, -3, -2).reshape(*lead, rows * cols // LANES, LANES)


def untiled(a, rows, cols):
    lead = a.shape[:-2]
    a = a.reshape(*lead, rows // SUB, cols // LANES, SUB, LANES)
    return jnp.swapaxes(a, -3, -2).reshape(*lead, rows, cols)


def shards(initial, depth, mask):
    bricks = lax.axis_size("brick")
    n, cols = depth.shape
    nj = cols // (SUB * LANES)
    row = (nj, SUB, LANES)
    f32 = jnp.float32
    initial, depth, mask = tiled(initial), tiled(depth), tiled(mask)
    tile = nj * SUB * SUB
    size = depth.shape[0]
    params = pltpu.CompilerParams(vmem_limit_bytes=VMEM_LIMIT)
    anywhere = pl.BlockSpec(memory_space=pl.ANY)
    local = pl.BlockSpec(memory_space=pltpu.VMEM)

    packed = pl.pallas_call(
        functools.partial(pack_kernel, nj),
        out_shape=jax.ShapeDtypeStruct((PACKED, *row), f32),
        in_specs=[anywhere] * 3,
        out_specs=local,
        scratch_shapes=[
            pltpu.VMEM((3, tile, LANES), f32),
            pltpu.VMEM((tile, LANES), f32),
            pltpu.VMEM((tile, LANES), jnp.int32),
            pltpu.SemaphoreType.DMA((3,)),
        ],
        compiler_params=params,
        name="pack",
    )(initial, depth, mask)

    up = [(2 * i, 2 * i + 3) for i in range(bricks - 1)]
    down = [(2 * i + 3, 2 * i + 1) for i in range(bricks - 1)]
    low1 = lax.ppermute(packed, ("brick", "cuts"), up)
    high1 = lax.ppermute(packed, ("brick", "cuts"), down)
    low0 = lax.ppermute(low1, "cuts", [(1, 0)])
    high0 = lax.ppermute(high1, "cuts", [(1, 0)])

    out, mid = pl.pallas_call(
        functools.partial(middle_kernel, nj, bricks),
        out_shape=[jax.ShapeDtypeStruct((3, size, LANES), f32), jax.ShapeDtypeStruct((2, MID, *row), f32)],
        in_specs=[local] * 3,
        out_specs=[local] * 2,
        scratch_shapes=[
            pltpu.VMEM((n, 3, *row), f32),
            pltpu.VMEM((n, 2, *row), f32),
            pltpu.VMEM((n, 3, *row), f32),
            pltpu.VMEM((n, 3, *row), f32),
            pltpu.VMEM((n // 2, 3, *row), f32),
            pltpu.VMEM((n // 2, 2, *row), f32),
            pltpu.VMEM((n // 2, 3, *row), f32),
            pltpu.VMEM((n, 3, *row), f32),
            pltpu.VMEM((n // 2, 3, *row), f32),
        ],
        compiler_params=params,
        cost_estimate=pl.CostEstimate(flops=60 * 5 * n * cols, bytes_accessed=10 * n * cols * 4, transcendentals=0),
        name="middle",
    )(initial, depth, mask)

    out = pl.pallas_call(
        functools.partial(edge_kernel, nj, bricks, n),
        out_shape=jax.ShapeDtypeStruct((3, size, LANES), f32),
        in_specs=[anywhere] * 6,
        out_specs=anywhere,
        scratch_shapes=[
            pltpu.VMEM((2, PACKED, *row), f32),
            pltpu.VMEM((2, MID, *row), f32),
            pltpu.VMEM((2, 3, tile, LANES), f32),
            pltpu.SemaphoreType.DMA((6,)),
        ],
        input_output_aliases={5: 0},
        compiler_params=params,
        name="edges",
    )(low1, high1, low0, high0, mid, out)
    return untiled(out, n, cols)[None]


def solution(mesh):
    placed = (P(None, ("grp", "brick"), None), P("brick", None), P("brick", None))
    return jax.shard_map(
        shards,
        mesh=mesh,
        in_specs=placed,
        out_specs=P("cuts", None, ("grp", "brick"), None),
        check_vma=False,
    )
```

profile of v0, /device:TPU:1, one launch (start us, length us, event | category | flops | bytes accessed | tf_op | source)
XLA Modules:
  0.0 48.0 jit_solution(7117152922055044148)
XLA Ops:
  0.0 0.0 copy-start
  0.0 1.5 %copy-done = f32[3,32,5120]{2,1,0:T(8,128)S(1)} copy-done((f32[3,32,5120]{2,1,0:T(8,128)S(1)}, f32[3,32,5120]{2,1,0:T(8,128)}, u32[]{:S(2)}) %copy-start) | copy-done | bytes 1966104
  1.5 0.0 copy-start.1
  1.5 1.1 %copy-done.1 = f32[32,5120]{1,0:T(8,128)S(1)} copy-done((f32[32,5120]{1,0:T(8,128)S(1)}, f32[32,5120]{1,0:T(8,128)}, u32[]{:S(2)}) %copy-start.1) | copy-done | bytes 655384
  2.6 0.0 copy-start.2
  2.6 1.1 %copy-done.2 = s32[32,5120]{1,0:T(8,128)S(1)} copy-done((s32[32,5120]{1,0:T(8,128)S(1)}, s32[32,5120]{1,0:T(8,128)}, u32[]{:S(2)}) %copy-start.2) | copy-done | bytes 655384
  3.7 0.6 %pack.1 = f32[19,5,8,128]{3,2,1,0:T(8,128)S(1)} custom-call(f32[3,1280,128]{2,1,0:T(8,128)S(1)} %bitcast.20, f32[1280,128]{1,0:T(8,128)S(1)} %bitcast.22, s32[1280,128]{1,0:T(8,128)S(1)} %bitcast.24), custom_call_target="tpu_custom_call" | custom-call | tf_op jit(solution)/shard_map/pack/pallas_call | solution.py:414
  4.4 1.3 %collective-permute-start.1 = (f32[19,5,8,128]{3,2,1,0:T(8,128)S(1)}, f32[19,5,8,128]{3,2,1,0:T(8,128)S(1)}, u32[]{:S(2)}, u32[]{:S(2)}) collective-permute-start(f32[19,5,8,128]{3,2,1,0:T(8,128)S(1)} %pack.1), channel_id=1, source_target_pairs={{3,1},{5,3},{7,5},{9,7},{11,9},{13,11},{15,13},{19,17},{21,19},{23... | collective-permute-start | bytes 1167368 | tf_op jit(solution)/shard_map/ppermute | solution.py:432
  5.7 0.7 %collective-permute-start = (f32[19,5,8,128]{3,2,1,0:T(8,128)S(1)}, f32[19,5,8,128]{3,2,1,0:T(8,128)S(1)}, u32[]{:S(2)}, u32[]{:S(2)}) collective-permute-start(f32[19,5,8,128]{3,2,1,0:T(8,128)S(1)} %pack.1), channel_id=1, source_target_pairs={{0,3},{2,5},{4,7},{6,9},{8,11},{10,13},{12,15},{16,19},{18,21},{20... | collective-permute-start | bytes 1167368 | tf_op jit(solution)/shard_map/ppermute | solution.py:431
  6.3 7.1 %collective-permute-done.1.high1 = f32[19,5,8,128]{3,2,1,0:T(8,128)S(1)} collective-permute-done((f32[19,5,8,128]{3,2,1,0:T(8,128)S(1)}, f32[19,5,8,128]{3,2,1,0:T(8,128)S(1)}, u32[]{:S(2)}, u32[]{:S(2)}) %collective-permute-start.1) | collective-permute-done | bytes 389152 | tf_op jit(solution)/shard_map/ppermute | solution.py:432
  13.4 1.3 %collective-permute-start.3 = (f32[19,5,8,128]{3,2,1,0:T(8,128)S(1)}, f32[19,5,8,128]{3,2,1,0:T(8,128)S(1)}, u32[]{:S(2)}, u32[]{:S(2)}) collective-permute-start(f32[19,5,8,128]{3,2,1,0:T(8,128)S(1)} %collective-permute-done.1.high1), channel_id=1, source_target_pairs={{1,0},{3,2},{5,4},{7,6},{9,8},{11,10},{13,12},{15,14},{17,16},{19,... | collective-permute-start | bytes 1167368 | tf_op jit(solution)/shard_map/ppermute | solution.py:434
  14.8 0.0 collective-permute-done.low1
  14.8 5.6 %collective-permute-start.2 = (f32[19,5,8,128]{3,2,1,0:T(8,128)S(1)}, f32[19,5,8,128]{3,2,1,0:T(8,128)S(1)}, u32[]{:S(2)}, u32[]{:S(2)}) collective-permute-start(f32[19,5,8,128]{3,2,1,0:T(8,128)S(1)} %collective-permute-done.low1), channel_id=1, source_target_pairs={{1,0},{3,2},{5,4},{7,6},{9,8},{11,10},{13,12},{15,14},{17,16},{19,... | collective-permute-start | bytes 1167368 | tf_op jit(solution)/shard_map/ppermute | solution.py:433
  20.4 21.9 %middle.1 = (f32[3,1280,128]{2,1,0:T(8,128)}, f32[2,46,5,8,128]{4,3,2,1,0:T(8,128)S(1)}) custom-call(f32[3,1280,128]{2,1,0:T(8,128)S(1)} %bitcast.21, f32[1280,128]{1,0:T(8,128)S(1)} %bitcast.23, s32[1280,128]{1,0:T(8,128)S(1)} %bitcast.25), custom_call_target="tpu_custom_call" | custom-call | flops 49152000 | bytes 6553600 | tf_op jit(solution)/shard_map/middle/pallas_call | solution.py:436
  42.3 0.0 collective-permute-done.3.high0
  42.3 0.0 collective-permute-done.2.low0
  42.3 5.7 %edges.1 = f32[3,1280,128]{2,1,0:T(8,128)} custom-call(f32[19,5,8,128]{3,2,1,0:T(8,128)S(1)} %collective-permute-done.low1, f32[19,5,8,128]{3,2,1,0:T(8,128)S(1)} %collective-permute-done.1.high1, f32[19,5,8,128]{3,2,1,0:T(8,128)S(1)} %collective-permute-done.2.low0, ...), custom_call_target="tpu_custom_call", output_to_operand_aliasing={{}: (5, {})} | custom-call | tf_op jit(solution)/shard_map/edges/pallas_call | solution.py:457
Async XLA Ops:
  0.0 1.5 %copy-start = (f32[3,32,5120]{2,1,0:T(8,128)S(1)}, f32[3,32,5120]{2,1,0:T(8,128)}, u32[]{:S(2)}) copy-start(f32[3,32,5120]{2,1,0:T(8,128)} %param.3) | copy-start | bytes 5898244
  1.5 1.1 %copy-start.1 = (f32[32,5120]{1,0:T(8,128)S(1)}, f32[32,5120]{1,0:T(8,128)}, u32[]{:S(2)}) copy-start(f32[32,5120]{1,0:T(8,128)} %param.4) | copy-start | bytes 1966084
  2.6 1.1 %copy-start.2 = (s32[32,5120]{1,0:T(8,128)S(1)}, s32[32,5120]{1,0:T(8,128)}, u32[]{:S(2)}) copy-start(s32[32,5120]{1,0:T(8,128)} %param.5) | copy-start | bytes 1966084
  4.4 9.1 %collective-permute-start.1 = (f32[19,5,8,128]{3,2,1,0:T(8,128)S(1)}, f32[19,5,8,128]{3,2,1,0:T(8,128)S(1)}, u32[]{:S(2)}, u32[]{:S(2)}) collective-permute-start(f32[19,5,8,128]{3,2,1,0:T(8,128)S(1)} %pack.1), channel_id=1, source_target_pairs={{3,1},{5,3},{7,5},{9,7},{11,9},{13,11},{15,13},{19,17},{21,19},{23... | collective-permute-start | bytes 1167368 | tf_op jit(solution)/shard_map/ppermute | solution.py:432
  5.7 9.1 %collective-permute-start = (f32[19,5,8,128]{3,2,1,0:T(8,128)S(1)}, f32[19,5,8,128]{3,2,1,0:T(8,128)S(1)}, u32[]{:S(2)}, u32[]{:S(2)}) collective-permute-start(f32[19,5,8,128]{3,2,1,0:T(8,128)S(1)} %pack.1), channel_id=1, source_target_pairs={{0,3},{2,5},{4,7},{6,9},{8,11},{10,13},{12,15},{16,19},{18,21},{20... | collective-permute-start | bytes 1167368 | tf_op jit(solution)/shard_map/ppermute | solution.py:431
  13.4 28.8 %collective-permute-start.3 = (f32[19,5,8,128]{3,2,1,0:T(8,128)S(1)}, f32[19,5,8,128]{3,2,1,0:T(8,128)S(1)}, u32[]{:S(2)}, u32[]{:S(2)}) collective-permute-start(f32[19,5,8,128]{3,2,1,0:T(8,128)S(1)} %collective-permute-done.1.high1), channel_id=1, source_target_pairs={{1,0},{3,2},{5,4},{7,6},{9,8},{11,10},{13,12},{15,14},{17,16},{19,... | collective-permute-start | bytes 1167368 | tf_op jit(solution)/shard_map/ppermute | solution.py:434
  14.8 27.5 %collective-permute-start.2 = (f32[19,5,8,128]{3,2,1,0:T(8,128)S(1)}, f32[19,5,8,128]{3,2,1,0:T(8,128)S(1)}, u32[]{:S(2)}, u32[]{:S(2)}) collective-permute-start(f32[19,5,8,128]{3,2,1,0:T(8,128)S(1)} %collective-permute-done.low1), channel_id=1, source_target_pairs={{1,0},{3,2},{5,4},{7,6},{9,8},{11,10},{13,12},{15,14},{17,16},{19,... | collective-permute-start | bytes 1167368 | tf_op jit(solution)/shard_map/ppermute | solution.py:433
where the time goes:
time: 48.3 us; the launch traced here: 48 us
  Pallas kernels  28.2 us (58%)
  starting transfers between devices  8.89 us (18%)
  waiting for transfers between devices  7.11 us (15%)
  local copies, waits for them, and re-layouts  3.72 us (8%)
    pallas_call x1, Pallas kernels, shards(): pl.pallas_call(functools.partial(middle_kernel, nj, bricks), out_shape=[j...  21.9 us
    ppermute x1, waiting for transfers between devices, shards(): high1 = lax.ppermute(packed, ('brick', 'cuts'), down)  7.1 us
    pallas_call x1, Pallas kernels, shards(): pl.pallas_call(functools.partial(edge_kernel, nj, bricks, n), out_shape=j...  5.69 us
    ppermute x1, starting transfers between devices, shards(): low0 = lax.ppermute(low1, 'cuts', [(1, 0)])  5.61 us
    unnamed x6, local copies, waits for them, and re-layouts  3.72 us
    ppermute x1, starting transfers between devices, shards(): high0 = lax.ppermute(high1, 'cuts', [(1, 0)])  1.3 us
    ppermute x1, starting transfers between devices, shards(): high1 = lax.ppermute(packed, ('brick', 'cuts'), down)  1.29 us
  transfers between devices with their start and end apart: 4, of which 1 were waited for; matrix products, arithmetic and copies ran while one was open for 0% of the time, Pallas kernels for 46%

commit v1 on v0

v1 whole, which is shorter than its diff:
```python
import functools

import jax
import jax.numpy as jnp
from jax import lax
from jax.experimental import pallas as pl
from jax.experimental.pallas import tpu as pltpu
from jax.sharding import PartitionSpec as P


COURANT = 0.2
DIFFUSION = 0.05
FRICTION = 0.01
CORIOLIS = 0.5
FINE_TIME = 0.2
COARSE_TIME = 0.4
SUB, LANES = 8, 128
HALO = 4
PER = 5
PACKED = HALO * PER - 1
VMEM_LIMIT = 24 * 1024 * 1024


def next_col(x, amount, edge):
    turned = [pltpu.roll(a, LANES - amount, 1) for a in x]
    turned.append(pltpu.roll(turned[0], SUB - 1, 0))
    return [jnp.where(edge, turned[j + 1], turned[j]) for j in range(len(x))]


def prev_col(x, amount, edge):
    turned = [pltpu.roll(a, amount, 1) for a in x]
    turned.insert(0, pltpu.roll(turned[-1], 1, 0))
    return [jnp.where(edge, turned[j], turned[j + 1]) for j in range(len(x))]


def lane_ids():
    return lax.broadcasted_iota(jnp.int32, (SUB, LANES), 1)


def each(f, *rows):
    return [f(*a) for a in zip(*rows)]


def steps(states, heights, wets, turns, dt, cols, beside=None):
    lane = lane_ids()
    last, first = lane >= LANES - cols, lane < cols
    k = (1.0 - dt * FRICTION - 4.0 * DIFFUSION) / DIFFUSION
    full = [each(jnp.add, h, s[0]) for h, s in zip(heights, states)]
    flux = [each(jnp.multiply, f, s[1]) for f, s in zip(full, states)]
    out = []
    for i, (wet, t) in enumerate(zip(wets, turns)):
        (eb, ub, vb), (e, u, v), (ea, ua, va) = states[i : i + 3]
        e_r, e_l = next_col(e, cols, last), prev_col(e, cols, first)
        u_r, u_l = next_col(u, cols, last), prev_col(u, cols, first)
        v_r, v_l = next_col(v, cols, last), prev_col(v, cols, first)
        if beside is None:
            cross = each(jnp.multiply, full[i + 1], v)
            g_r, g_l = next_col(cross, cols, last), prev_col(cross, cols, first)
        else:
            g_r, g_l = (each(lambda h, a, b: (h + a) * b, *x) for x in zip(beside[i], (e_r, e_l), (v_r, v_l)))
        new_e, new_u, new_v = [], [], []
        for j in range(len(e)):
            spread = ((ea[j] - flux[i + 2][j]) + (eb[j] + flux[i][j])) + ((e_r[j] - g_r[j]) + (e_l[j] + g_l[j]))
            new_e.append(DIFFUSION * (e[j] * (1.0 / DIFFUSION - 4.0) + spread))
            nu = u[j] * (k - (ua[j] - ub[j])) + v[j] * (t - (u_r[j] - u_l[j]))
            nu = nu + (((ua[j] - ea[j]) + (ub[j] + eb[j])) + (u_r[j] + u_l[j]))
            nv = v[j] * (k - (v_r[j] - v_l[j])) - u[j] * (t + (va[j] - vb[j]))
            nv = nv + (((v_r[j] - e_r[j]) + (v_l[j] + e_l[j])) + (va[j] + vb[j]))
            new_u.append(nu * wet[j])
            new_v.append(nv * wet[j])
        out.append((new_e, new_u, new_v))
    return out


def average(low, high):
    even = lane_ids() % 2 == 0

    def one(a, b):
        s = a + b
        return (s + jnp.where(even, pltpu.roll(s, LANES - 1, 1), pltpu.roll(s, 1, 1))) * 0.25

    return each(one, low, high)


def average3(low, high):
    return tuple(average(a, b) for a, b in zip(low, high))


def interleave(x, y):
    even = lane_ids() % 2 == 0
    return tuple(each(lambda a, b: jnp.where(even, a, b), p, q) for p, q in zip(x, y))


def difference(z):
    even = lane_ids() % 2 == 0
    one = lambda a: jnp.where(even, a - pltpu.roll(a, LANES - 1, 1), pltpu.roll(a, 1, 1) - a)
    return tuple(each(one, row) for row in z)


def added(x, y):
    return tuple(each(jnp.add, a, b) for a, b in zip(x, y))


def rows_of(ref, *at):
    return [ref[(*at, j)] for j in range(ref.shape[-3])]


def put(ref, at, row):
    for j, a in enumerate(row):
        ref[(*at, j)] = a


def three(ref, at):
    return tuple(rows_of(ref, at, k) for k in range(3))


def put_three(ref, at, rows):
    for k, row in enumerate(rows):
        put(ref, (at, k), row)


def masked(rows, factor):
    e, u, v = rows
    return [a * factor for a in e], u, v


def turning(row, first_row, scale, all_rows, dt):
    y = (first_row + row).astype(jnp.float32) * (2.0 * scale) + scale
    return (dt * CORIOLIS / DIFFUSION) * (y * (1.0 / all_rows) - 1.0)


def in_tiles(nj, row, j):
    tile = nj * SUB * SUB
    return pl.ds((row // SUB) * tile + row % SUB + j * SUB, SUB, stride=nj * SUB)


SCALE = (4.0, 2.0, 2.0)


def emit(ref, at, nj, row, rows):
    for k in range(3):
        for j in range(nj):
            ref[(*at, k, in_tiles(nj, row, j))] = rows[k][j] * (1.0 / SCALE[k])


def wetness(mask):
    return mask.astype(jnp.float32) * DIFFUSION


def pack_kernel(nj, initial, depth, mask, out, initial_v, depth_v, mask_v, sems):
    lane = lax.axis_index("cuts")
    tile = nj * SUB * SUB
    high = initial.shape[1] // tile - 1
    start = pl.multiple_of(jnp.where(lane == 0, 0, high) * tile, tile)
    copies = [
        pltpu.make_async_copy(initial.at[:, pl.ds(start, tile), :], initial_v, sems.at[0]),
        pltpu.make_async_copy(depth.at[pl.ds(start, tile), :], depth_v, sems.at[1]),
        pltpu.make_async_copy(mask.at[pl.ds(start, tile), :], mask_v, sems.at[2]),
    ]
    for copy in copies:
        copy.start()
    for copy in copies:
        copy.wait()

    def fill(row_of):
        for d in range(HALO):
            for j in range(nj):
                at = in_tiles(nj, row_of(d), j)
                for k in range(3):
                    out[d * PER + k, j] = initial_v[k, at, :] * SCALE[k]
                out[d * PER + 3, j] = depth_v[at, :] * 4.0
                if d < HALO - 1:
                    out[d * PER + 4, j] = wetness(mask_v[at, :])

    pl.when(lane == 0)(lambda: fill(lambda d: d))
    pl.when(lane != 0)(lambda: fill(lambda d: SUB - 1 - d))


def loop(low, high, most, body):
    count = max(c for c in range(1, most + 1) if (high - low) % c == 0)

    def run(i, carry):
        body(low + i * count, count)
        return carry

    if high - low == count:
        body(low, count)
        return
    lax.fori_loop(0, (high - low) // count, run, 0)


def sideways(h):
    lane = lane_ids()
    return next_col(h, 1, lane >= LANES - 1), prev_col(h, 1, lane < 1)


def middle_kernel(nj, bricks, initial, depth, mask, out, ini, hw, s1, rc, c1, p1, tiles, s2, rhw, dif, sems):
    lane = lax.axis_index("cuts")
    brick = lax.axis_index("brick")
    n = ini.shape[0]
    m = n // 2
    all_rows = n * bricks
    tile = nj * SUB * SUB
    parts = n // SUB

    def load(t, carry):
        for r in range(SUB):
            row = t * SUB + r
            high = []
            for j in range(nj):
                at = pl.ds(t * tile + r + j * SUB, SUB, stride=nj * SUB)
                for k in range(3):
                    ini[row, k, j] = initial[k, at, :] * SCALE[k]
                high.append(depth[at, :] * 4.0)
                hw[row, 1, j] = wetness(mask[at, :])
            put(hw, (row, 0), high)
            for k, side in enumerate(sideways(high)):
                put(hw, (row, 2 + k), side)
        return carry

    lax.fori_loop(0, parts, load, 0)

    def fine(states, row, count):
        return steps(
            states,
            [rows_of(hw, row + d, 0) for d in range(-1, count + 1)],
            [rows_of(hw, row + d, 1) for d in range(count)],
            [turning(row + d, brick * n, 1.0, all_rows, FINE_TIME) for d in range(count)],
            FINE_TIME,
            1,
            [(rows_of(hw, row + d, 2), rows_of(hw, row + d, 3)) for d in range(count)],
        )

    def around(ref, row, count):
        return [three(ref, row + d) for d in range(-1, count + 1)]

    def coarse(states, row, count):
        return steps(
            states,
            [rows_of(rhw, row + d, 0) for d in range(-1, count + 1)],
            [rows_of(rhw, row + d, 1) for d in range(count)],
            [turning(row + d, brick * m, 2.0, all_rows, COARSE_TIME) for d in range(count)],
            COARSE_TIME,
            2,
        )

    def store(ref, row, new):
        for d, rows in enumerate(new):
            put_three(ref, row + d, rows)

    def send(t):
        at = pl.ds(t * tile, tile)
        return pltpu.make_async_copy(tiles.at[:, at, :], out.at[:, at, :], sems.at[t])

    def emitted(first, rows_at):
        for t in range(parts):
            low, high = max(first, t * SUB), min(n - first, (t + 1) * SUB)
            loop(low, high, 4, rows_at)
            send(t).start()
        for t in range(parts):
            send(t).wait()

    loop(1, n - 1, 5, lambda row, c: store(s1, row, fine(around(ini, row, c), row, c)))
    loop(2, n - 2, 4, lambda row, c: store(s2, row, fine(around(s1, row, c), row, c)))

    @pl.when(lane == 0)
    def _():
        def copied(row, count):
            for d in range(count):
                emit(tiles, (), nj, row + d, three(s2, row + d))

        emitted(2, copied)

    @pl.when(lane != 0)
    def _():
        def restrict(row, count):
            for d in range(count):
                low, high = 2 * (row + d), 2 * (row + d) + 1
                put_three(rc, row + d, average3(three(ini, low), three(ini, high)))
                for k in range(2):
                    put(rhw, (row + d, k), average(rows_of(hw, low, k), rows_of(hw, high, k)))

        loop(0, m, 4, restrict)
        loop(1, m - 1, 7, lambda row, c: store(c1, row, coarse(around(rc, row, c), row, c)))

        def again(row, count):
            for d in range(count):
                low, high = 2 * (row + d), 2 * (row + d) + 1
                put_three(rc, row + d, average3(three(s2, low), three(s2, high)))

        loop(1, m - 1, 7, again)

        def correct(row, count):
            both = [interleave(a, b) for a, b in zip(around(rc, row, count), around(c1, row, count))]
            store(dif, row, [difference(z) for z in coarse(both, row, count)])

        loop(2, m - 2, 4, correct)

        def prolonged(half, count):
            row = 2 * half + 1
            pairs = [three(c1, half + d) for d in range(count + 1)]
            store(p1, row, fine([pairs[d // 2] for d in range(2 * count + 2)], row, 2 * count))

        loop(1, m - 2, 2, prolonged)

        def last(row, count):
            for d, rows in enumerate(fine(around(p1, row, count), row, count)):
                emit(tiles, (), nj, row + d, added(rows, three(dif, (row + d) // 2)))

        emitted(4, last)


def edge_kernel(nj, bricks, n, turned, near, ini, hw, s1, rf, c1, p1, before, out, tiles, sems):
    lane = lax.axis_index("cuts")
    brick = lax.axis_index("brick")
    all_rows = n * bricks
    m = n // 2
    wide = nj * SUB

    def own(s, i, count):
        return i if s == 0 else count - 1 - i

    def depth(s, i):
        return rows_of(near, (-1 - i) * PER + 3) if i < 0 else rows_of(hw, own(s, i, n), 0)

    def wet(s, i):
        return rows_of(near, (-1 - i) * PER + 4) if i < 0 else rows_of(hw, own(s, i, n), 1)

    def initial(s, i):
        if i < 0:
            return tuple(rows_of(near, (-1 - i) * PER + k) for k in range(3))
        return three(ini, own(s, i, n))

    def known(ref, s, ids):
        return {i: three(ref, own(s, i, ref.shape[0])) for i in ids}

    def inside(s):
        there = brick > 0 if s == 0 else brick < bricks - 1
        return jnp.where(there, 1.0, 0.0).astype(jnp.float32)

    def advance(s, ids, state, heights, wets, turn, dt, cols, beside=None):
        run = list(ids) if s == 0 else list(ids)[::-1]
        way = 1 if s == 0 else -1
        span = [run[0] - way, *run, run[-1] + way]
        sides = None if beside is None else [beside(i) for i in run]
        new = steps([state(i) for i in span], [heights(i) for i in span], [wets(i) for i in run], [turn(i) for i in run], dt, cols, sides)
        return {i: masked(x, inside(s)) if i < 0 else x for i, x in zip(run, new)}

    def fine(s, ids, state, beside):
        turn = lambda i: turning(jnp.int32(own(s, i, n)), brick * n, 1.0, all_rows, FINE_TIME)
        return advance(s, ids, state, lambda i: depth(s, i), lambda i: wet(s, i), turn, FINE_TIME, 1, beside)

    def coarse(s, ids, state, deep, dry):
        turn = lambda i: turning(jnp.int32(own(s, i, m)), brick * m, 2.0, all_rows, COARSE_TIME)
        return advance(s, ids, state, deep.__getitem__, dry.__getitem__, turn, COARSE_TIME, 2)

    def sides_from(s, outer):
        held = {i: sideways(depth(s, i)) for i in range(outer, 0)}
        return lambda i: held[i] if i < 0 else (rows_of(hw, own(s, i, n), 2), rows_of(hw, own(s, i, n), 3))

    def flown(s, outer, beside):
        one = fine(s, range(outer - 1, 1), lambda i: initial(s, i), beside)
        one.update(known(s1, s, (1, 2)))
        return fine(s, range(outer, 2), one.__getitem__, beside)

    def send(s, rows):
        count = len(rows)
        for i, x in rows.items():
            emit(tiles, (), nj, own(s, i, SUB), x)
        at = 0 if s == 0 else SUB - count
        where = 0 if s == 0 else (n // SUB - 1) * wide
        src = tiles.reshape(3, wide, SUB, LANES).at[:, :, at : at + count, :]
        copy = pltpu.make_async_copy(src, out.at[:, where : where + wide, at : at + count, :], sems.at[0])
        copy.start()
        copy.wait()

    @pl.when(lane == 0)
    def _():
        s = int(turned)
        send(s, {i: x for i, x in flown(s, 0, sides_from(s, -1)).items() if i >= 0})

    @pl.when(lane != 0)
    def _():
        s = 1 - int(turned)
        beside = sides_from(s, -3)
        two = flown(s, -2, beside)
        fresh = {i: average3(two[2 * i], two[2 * i + 1]) for i in (-1, 0)}
        fresh.update(known(rf, s, (1, 2)))
        start = {i: average3(initial(s, 2 * i), initial(s, 2 * i + 1)) for i in range(-2, 2)}
        deep = {i: average(depth(s, 2 * i), depth(s, 2 * i + 1)) for i in range(-2, 3)}
        dry = {i: average(wet(s, 2 * i), wet(s, 2 * i + 1)) for i in (-1, 0, 1)}
        first = coarse(s, (-1, 0), start.__getitem__, deep, dry)
        first.update(known(c1, s, (1, 2)))
        both = {i: interleave(fresh[i], first[i]) for i in range(-1, 3)}
        add = {i: difference(z) for i, z in coarse(s, (0, 1), both.__getitem__, deep, dry).items()}
        one = fine(s, range(-1, 3), lambda i: first[i // 2], beside)
        one.update(known(p1, s, (3, 4)))
        send(s, {i: added(x, add[i // 2]) for i, x in fine(s, range(4), one.__getitem__, beside).items()})


def tiled(a):
    *lead, rows, cols = a.shape
    a = a.reshape(*lead, rows // SUB, SUB, cols // LANES, LANES)
    return jnp.swapaxes(a, -3, -2).reshape(*lead, rows * cols // LANES, LANES)


def untiled(a, rows, cols):
    lead = a.shape[:-2]
    a = a.reshape(*lead, rows // SUB, cols // LANES, SUB, LANES)
    return jnp.swapaxes(a, -3, -2).reshape(*lead, rows, cols)


def shards(initial, depth, mask):
    bricks = lax.axis_size("brick")
    n, cols = depth.shape
    nj = cols // (SUB * LANES)
    row = (nj, SUB, LANES)
    f32 = jnp.float32
    initial, depth, mask = tiled(initial), tiled(depth), tiled(mask)
    tile = nj * SUB * SUB
    size = depth.shape[0]
    params = pltpu.CompilerParams(vmem_limit_bytes=VMEM_LIMIT)
    far = pl.BlockSpec(memory_space=pltpu.HBM)
    local = pl.BlockSpec(memory_space=pltpu.VMEM)

    def hold(rows, count):
        return jax.ShapeDtypeStruct((rows, count, *row), f32)

    packed = pl.pallas_call(
        functools.partial(pack_kernel, nj),
        out_shape=jax.ShapeDtypeStruct((PACKED, *row), f32),
        in_specs=[far] * 3,
        out_specs=local,
        scratch_shapes=[
            pltpu.VMEM((3, tile, LANES), f32),
            pltpu.VMEM((tile, LANES), f32),
            pltpu.VMEM((tile, LANES), jnp.int32),
            pltpu.SemaphoreType.DMA((3,)),
        ],
        compiler_params=params,
        name="pack",
    )(*(pltpu.with_memory_space_constraint(a, pltpu.HBM) for a in (initial, depth, mask)))

    up = [(2 * i + 1, 2 * i + 2) for i in range(bricks - 1)]
    near = lax.ppermute(packed, ("brick", "cuts"), up + [(b, a) for a, b in up])

    whole, *held = pl.pallas_call(
        functools.partial(middle_kernel, nj, bricks),
        out_shape=[
            jax.ShapeDtypeStruct((3, size, LANES), f32),
            hold(n, 3),
            hold(n, 4),
            hold(n, 3),
            hold(n // 2, 3),
            hold(n // 2, 3),
            hold(n, 3),
        ],
        in_specs=[local] * 3,
        out_specs=[far] + [local] * 6,
        scratch_shapes=[
            pltpu.VMEM((3, size, LANES), f32),
            pltpu.VMEM((n, 3, *row), f32),
            pltpu.VMEM((n // 2, 2, *row), f32),
            pltpu.VMEM((n // 2, 3, *row), f32),
            pltpu.SemaphoreType.DMA((n // SUB,)),
        ],
        compiler_params=params,
        cost_estimate=pl.CostEstimate(flops=60 * 5 * n * cols, bytes_accessed=10 * n * cols * 4, transcendentals=0),
        name="middle",
    )(initial, depth, mask)

    def edges(turned, near, before):
        return pl.pallas_call(
            functools.partial(edge_kernel, nj, bricks, n, turned),
            out_shape=jax.ShapeDtypeStruct((3, size // SUB, SUB, LANES), f32),
            in_specs=[local] * 7 + [far],
            out_specs=far,
            scratch_shapes=[pltpu.VMEM((3, tile, LANES), f32), pltpu.SemaphoreType.DMA((1,))],
            input_output_aliases={7: 0},
            compiler_params=params,
            cost_estimate=pl.CostEstimate(flops=60 * n * cols, bytes_accessed=n * cols * 4, transcendentals=0),
            name="edges",
        )(near, *held, before)

    near, *held = lax.optimization_barrier((near, *held))
    other = lax.ppermute(near, "cuts", [(0, 1), (1, 0)])
    whole = edges(False, near, whole.reshape(3, size // SUB, SUB, LANES))
    whole = edges(True, other, whole)
    return untiled(whole.reshape(3, size, LANES), n, cols)[None]


def solution(mesh):
    placed = (P(None, ("grp", "brick"), None), P("brick", None), P("brick", None))
    return jax.shard_map(
        shards,
        mesh=mesh,
        in_specs=placed,
        out_specs=P("cuts", None, ("grp", "brick"), None),
        check_vma=False,
    )
```

time: 48.3 us -> 22.5 us (0.47)
  Pallas kernels: 28.2 us -> 17.7 us
  waiting for transfers between devices: 7.11 us -> 0.01 us
  starting transfers between devices: 8.89 us -> 4.61 us
  local copies, waits for them, and re-layouts: 3.72 us -> 0.01 us
    pallas_call x1, Pallas kernels: 21.9 us -> 12 us  [shards(): pl.pallas_call(functools.partial(middle_kernel, nj, bricks), out_shape=[j...]
    ppermute x4 -> x2, waiting for transfers between devices: 7.11 us -> 0.01 us  [the longest x1 0.01 us: shards(): near = lax.ppermute(packed, ('brick', 'cuts'), up + [(b, a) for a, b in up])]
    ppermute x4 -> x2, starting transfers between devices: 8.89 us -> 4.61 us  [the longest x1 4.54 us: shards(): near = lax.ppermute(packed, ('brick', 'cuts'), up + [(b, a) for a, b in up])]
    unnamed x6, local copies, waits for them, and re-layouts: 3.72 us -> 0.01 us
    pallas_call x1 -> x2, Pallas kernels: 5.69 us -> 4.28 us  [edges(): pl.pallas_call(functools.partial(edge_kernel, nj, bricks, n, turned), out...]
    pallas_call x1, Pallas kernels: 0.63 us -> 1.41 us  [shards(): pl.pallas_call(functools.partial(pack_kernel, nj), out_shape=jax.ShapeDty...]
  transfers between devices with their start and end apart: 4 -> 2, of which waited for: 1 -> 0; matrix products, arithmetic and copies ran while one was open for 0% -> 0% of each run, Pallas kernels for 46% -> 63%
where the time goes in v1:
time: 22.5 us; the launch traced here: 22.4 us
  Pallas kernels  17.7 us (79%)
  starting transfers between devices  4.61 us (20%)
    pallas_call x1, Pallas kernels, shards(): pl.pallas_call(functools.partial(middle_kernel, nj, bricks), out_shape=[j...  12 us
    ppermute x1, starting transfers between devices, shards(): near = lax.ppermute(packed, ('brick', 'cuts'), up + [(b, a) for a, b in up])  4.54 us
    pallas_call x2, Pallas kernels, edges(): pl.pallas_call(functools.partial(edge_kernel, nj, bricks, n, turned), out...  4.28 us
    pallas_call x1, Pallas kernels, shards(): pl.pallas_call(functools.partial(pack_kernel, nj), out_shape=jax.ShapeDty...  1.41 us
  transfers between devices with their start and end apart: 2, of which 0 were waited for; matrix products, arithmetic and copies ran while one was open for 0% of the time, Pallas kernels for 63%

profile of v1, /device:TPU:1, one launch (start us, length us, event | category | flops | bytes accessed | tf_op | source)
XLA Modules:
  0.0 22.4 jit_solution(13627011425769338273)
XLA Ops:
  0.0 0.0 copy-start.2
  0.0 0.0 copy-start.1
  0.0 0.0 copy-start
  0.0 1.4 %pack.1 = f32[19,5,8,128]{3,2,1,0:T(8,128)S(1)} custom-call(f32[3,1280,128]{2,1,0:T(8,128)} %bitcast.21, f32[1280,128]{1,0:T(8,128)} %bitcast.23, s32[1280,128]{1,0:T(8,128)} %bitcast.25), custom_call_target="tpu_custom_call" | custom-call | tf_op jit(solution)/shard_map/pack/pallas_call | solution.py:429
  1.4 4.5 %collective-permute-start = (f32[19,5,8,128]{3,2,1,0:T(8,128)S(1)}, f32[19,5,8,128]{3,2,1,0:T(8,128)S(1)}, u32[]{:S(2)}, u32[]{:S(2)}) collective-permute-start(f32[19,5,8,128]{3,2,1,0:T(8,128)S(1)} %pack.1), channel_id=1, source_target_pairs={{1,2},{3,4},{5,6},{7,8},{9,10},{11,12},{13,14},{2,1},{4,3},{6,5},{... | collective-permute-start | bytes 1167368 | tf_op jit(solution)/shard_map/ppermute | solution.py:445
  6.0 0.0 copy-done.2
  6.0 0.0 copy-done.1
  6.0 0.0 copy-done
  6.0 12.0 %middle.1 = (f32[3,1280,128]{2,1,0:T(8,128)}, f32[32,3,5,8,128]{4,3,2,1,0:T(8,128)S(1)}, f32[32,4,5,8,128]{4,3,2,1,0:T(8,128)S(1)}, f32[32,3,5,8,128]{4,3,2,1,0:...) custom-call(f32[3,1280,128]{2,1,0:T(8,128)S(1)} %bitcast.22, ...), custom_call_target="tpu_custom_call" | custom-call | flops 49152000 | bytes 6553600 | tf_op jit(solution)/shard_map/middle/pallas_call | solution.py:447
  18.0 0.0 collective-permute-done.near
  18.0 0.1 collective-permute-start.1
  18.1 2.1 %edges.2.before = f32[3,160,8,128]{3,2,1,0:T(8,128)} custom-call(f32[19,5,8,128]{3,2,1,0:T(8,128)S(1)} %collective-permute-done.near, f32[32,3,5,8,128]{4,3,2,1,0:T(8,128)S(1)} %get-tuple-element.26.ini, f32[32,4,5,8,128]{4,3,2,1,0:T(8,128)S(1)} %get-tuple-element.27.hw, ...), custom_call_target="tpu_custom_call", output_to_operand_aliasing={{}: (7, {})} | custom-call | flops 9830400 | bytes 655360 | tf_op jit(solution)/shard_map/edges/pallas_call | solution.py:473
  20.2 0.0 collective-permute-done.1.near
  20.2 2.2 %edges.3 = f32[3,160,8,128]{3,2,1,0:T(8,128)} custom-call(f32[19,5,8,128]{3,2,1,0:T(8,128)S(1)} %collective-permute-done.1.near, f32[32,3,5,8,128]{4,3,2,1,0:T(8,128)S(1)} %get-tuple-element.26.ini, f32[32,4,5,8,128]{4,3,2,1,0:T(8,128)S(1)} %get-tuple-element.27.hw, f32[32,3,5,8,128]{4,3,2,1,0:T(8,128)S(1)} %get-tuple-element.28.s1, ...), custom_call_target="tpu_custom_call", output_to_operand_aliasing={{}: (7, {})} | custom-call | flops 9830400 | bytes 655360 | tf_op jit(solution)/shard_map/edges/pallas_call | solution.py:473
Async XLA Ops:
  0.0 6.0 %copy-start.2 = (s32[32,5120]{1,0:T(8,128)S(1)}, s32[32,5120]{1,0:T(8,128)}, u32[]{:S(2)}) copy-start(s32[32,5120]{1,0:T(8,128)} %param.5) | copy-start | bytes 1966084
  0.0 6.0 %copy-start.1 = (f32[32,5120]{1,0:T(8,128)S(1)}, f32[32,5120]{1,0:T(8,128)}, u32[]{:S(2)}) copy-start(f32[32,5120]{1,0:T(8,128)} %param.4) | copy-start | bytes 1966084
  0.0 6.0 %copy-start = (f32[3,32,5120]{2,1,0:T(8,128)S(1)}, f32[3,32,5120]{2,1,0:T(8,128)}, u32[]{:S(2)}) copy-start(f32[3,32,5120]{2,1,0:T(8,128)} %param.3) | copy-start | bytes 5898244
  1.4 16.6 %collective-permute-start = (f32[19,5,8,128]{3,2,1,0:T(8,128)S(1)}, f32[19,5,8,128]{3,2,1,0:T(8,128)S(1)}, u32[]{:S(2)}, u32[]{:S(2)}) collective-permute-start(f32[19,5,8,128]{3,2,1,0:T(8,128)S(1)} %pack.1), channel_id=1, source_target_pairs={{1,2},{3,4},{5,6},{7,8},{9,10},{11,12},{13,14},{2,1},{4,3},{6,5},{... | collective-permute-start | bytes 1167368 | tf_op jit(solution)/shard_map/ppermute | solution.py:445
  18.0 2.2 %collective-permute-start.1 = (f32[19,5,8,128]{3,2,1,0:T(8,128)S(1)}, f32[19,5,8,128]{3,2,1,0:T(8,128)S(1)}, u32[]{:S(2)}, u32[]{:S(2)}) collective-permute-start(f32[19,5,8,128]{3,2,1,0:T(8,128)S(1)} %collective-permute-done.near), channel_id=1, source_target_pairs={{0,1},{1,0},{2,3},{3,2},{4,5},{5,4},{6,7},{7,6},{8,9},{9,8},{10,11... | collective-permute-start | bytes 1167368 | tf_op jit(solution)/shard_map/ppermute | solution.py:486

commit v2 on v1

v2 whole, which is shorter than its diff:
```python
import functools

import jax
import jax.numpy as jnp
from jax import lax
from jax.experimental import pallas as pl
from jax.experimental.pallas import tpu as pltpu
from jax.sharding import PartitionSpec as P


COURANT = 0.2
DIFFUSION = 0.05
FRICTION = 0.01
CORIOLIS = 0.5
FINE_TIME = 0.2
COARSE_TIME = 0.4
SUB, LANES = 8, 128
HALO = 4
PER = 5
PACKED = HALO * PER - 1
VMEM_LIMIT = 24 * 1024 * 1024


def next_col(x, amount, edge):
    turned = [pltpu.roll(a, LANES - amount, 1) for a in x]
    turned.append(pltpu.roll(turned[0], SUB - 1, 0))
    return [jnp.where(edge, turned[j + 1], turned[j]) for j in range(len(x))]


def prev_col(x, amount, edge):
    turned = [pltpu.roll(a, amount, 1) for a in x]
    turned.insert(0, pltpu.roll(turned[-1], 1, 0))
    return [jnp.where(edge, turned[j], turned[j + 1]) for j in range(len(x))]


def lane_ids():
    return lax.broadcasted_iota(jnp.int32, (SUB, LANES), 1)


def each(f, *rows):
    return [f(*a) for a in zip(*rows)]


def steps(states, heights, wets, turns, dt, cols, beside):
    lane = lane_ids()
    last, first = lane >= LANES - cols, lane < cols
    k = (1.0 - dt * FRICTION - 4.0 * DIFFUSION) / DIFFUSION
    full = [each(jnp.add, h, s[0]) for h, s in zip(heights, states)]
    flux = [each(jnp.multiply, f, s[1]) for f, s in zip(full, states)]
    out = []
    shifted = None
    for i, (wet, t) in enumerate(zip(wets, turns)):
        (eb, ub, vb), (e, u, v), (ea, ua, va) = states[i : i + 3]
        if shifted is None or states[i + 1] is not states[i]:
            shifted = [(next_col(a, cols, last), prev_col(a, cols, first)) for a in (e, u, v)]
        (e_r, e_l), (u_r, u_l), (v_r, v_l) = shifted
        g_r, g_l = (each(lambda h, a, b: (h + a) * b, *x) for x in zip(beside[i], (e_r, e_l), (v_r, v_l)))
        new_e, new_u, new_v = [], [], []
        for j in range(len(e)):
            spread = ((ea[j] - flux[i + 2][j]) + (eb[j] + flux[i][j])) + ((e_r[j] - g_r[j]) + (e_l[j] + g_l[j]))
            new_e.append(DIFFUSION * (e[j] * (1.0 / DIFFUSION - 4.0) + spread))
            nu = u[j] * (k - (ua[j] - ub[j])) + v[j] * (t - (u_r[j] - u_l[j]))
            nu = nu + (((ua[j] - ea[j]) + (ub[j] + eb[j])) + (u_r[j] + u_l[j]))
            nv = v[j] * (k - (v_r[j] - v_l[j])) - u[j] * (t + (va[j] - vb[j]))
            nv = nv + (((v_r[j] - e_r[j]) + (v_l[j] + e_l[j])) + (va[j] + vb[j]))
            new_u.append(nu * wet[j])
            new_v.append(nv * wet[j])
        out.append((new_e, new_u, new_v))
    return out


def average(low, high):
    even = lane_ids() % 2 == 0

    def one(a, b):
        s = a + b
        return (s + jnp.where(even, pltpu.roll(s, LANES - 1, 1), pltpu.roll(s, 1, 1))) * 0.25

    return each(one, low, high)


def average3(low, high):
    return tuple(average(a, b) for a, b in zip(low, high))


def interleave(x, y):
    even = lane_ids() % 2 == 0
    return tuple(each(lambda a, b: jnp.where(even, a, b), p, q) for p, q in zip(x, y))


def difference(z):
    even = lane_ids() % 2 == 0
    one = lambda a: jnp.where(even, a - pltpu.roll(a, LANES - 1, 1), pltpu.roll(a, 1, 1) - a)
    return tuple(each(one, row) for row in z)


def added(x, y):
    return tuple(each(jnp.add, a, b) for a, b in zip(x, y))


def rows_of(ref, *at):
    return [ref[(*at, j)] for j in range(ref.shape[-3])]


def put(ref, at, row):
    for j, a in enumerate(row):
        ref[(*at, j)] = a


def three(ref, at):
    return tuple(rows_of(ref, at, k) for k in range(3))


def put_three(ref, at, rows):
    for k, row in enumerate(rows):
        put(ref, (at, k), row)


def masked(rows, factor):
    e, u, v = rows
    return [a * factor for a in e], u, v


def turning(row, first_row, scale, all_rows, dt):
    y = (first_row + row).astype(jnp.float32) * (2.0 * scale) + scale
    return (dt * CORIOLIS / DIFFUSION) * (y * (1.0 / all_rows) - 1.0)


def in_tiles(nj, row, j):
    tile = nj * SUB * SUB
    return pl.ds((row // SUB) * tile + row % SUB + j * SUB, SUB, stride=nj * SUB)


SCALE = (4.0, 2.0, 2.0)


def emit(ref, at, nj, row, rows):
    for k in range(3):
        for j in range(nj):
            ref[(*at, k, in_tiles(nj, row, j))] = rows[k][j] * (1.0 / SCALE[k])


def wetness(mask):
    return mask.astype(jnp.float32) * DIFFUSION


def pack_kernel(nj, initial, depth, mask, out, initial_v, depth_v, mask_v, sems):
    lane = lax.axis_index("cuts")
    wide = nj * SUB

    def fill(tile, at, row_of):
        there = pl.ds(tile, wide), pl.ds(at, HALO)
        copies = [
            pltpu.make_async_copy(initial.at[:, *there, :], initial_v, sems.at[0]),
            pltpu.make_async_copy(depth.at[*there, :], depth_v, sems.at[1]),
            pltpu.make_async_copy(mask.at[*there, :], mask_v, sems.at[2]),
        ]
        for copy in copies:
            copy.start()
        for copy in copies:
            copy.wait()
        flat = [ref.reshape(*ref.shape[:-3], wide * HALO, LANES) for ref in (initial_v, depth_v, mask_v)]
        for d in range(HALO):
            for j in range(nj):
                at = pl.ds(row_of(d) + j * HALO, SUB, stride=nj * HALO)
                for k in range(3):
                    out[d * PER + k, j] = flat[0][k, at, :] * SCALE[k]
                out[d * PER + 3, j] = flat[1][at, :] * 4.0
                if d < HALO - 1:
                    out[d * PER + 4, j] = wetness(flat[2][at, :])

    pl.when(lane == 0)(lambda: fill(0, 0, lambda d: d))
    pl.when(lane != 0)(lambda: fill(depth.shape[0] - wide, SUB - HALO, lambda d: HALO - 1 - d))


def loop(low, high, count, body):
    times, rest = divmod(high - low, count)

    def run(i, carry):
        body(low + i * count, count)
        return carry

    if times > 1:
        lax.fori_loop(0, times, run, 0)
    elif times:
        body(low, count)
    if rest:
        body(high - rest, rest)


def sideways(h, cols):
    lane = lane_ids()
    return next_col(h, cols, lane >= LANES - cols), prev_col(h, cols, lane < cols)


def middle_kernel(nj, bricks, initial, depth, mask, tiles, ini, hw, s1, rc, rhw, rf, c1, p1, s2, dif):
    lane = lax.axis_index("cuts")
    brick = lax.axis_index("brick")
    n = ini.shape[0]
    m = n // 2
    all_rows = n * bricks
    tile = nj * SUB * SUB
    parts = n // SUB

    def load(t, carry):
        for r in range(SUB):
            row = t * SUB + r
            high = []
            for j in range(nj):
                at = pl.ds(t * tile + r + j * SUB, SUB, stride=nj * SUB)
                for k in range(3):
                    ini[row, k, j] = initial[k, at, :] * SCALE[k]
                high.append(depth[at, :] * 4.0)
                hw[row, 1, j] = wetness(mask[at, :])
            put(hw, (row, 0), high)
            for k, side in enumerate(sideways(high, 1)):
                put(hw, (row, 2 + k), side)
        return carry

    lax.fori_loop(0, parts, load, 0)

    def fine(states, row, count):
        return steps(
            states,
            [rows_of(hw, row + d, 0) for d in range(-1, count + 1)],
            [rows_of(hw, row + d, 1) for d in range(count)],
            [turning(row + d, brick * n, 1.0, all_rows, FINE_TIME) for d in range(count)],
            FINE_TIME,
            1,
            [(rows_of(hw, row + d, 2), rows_of(hw, row + d, 3)) for d in range(count)],
        )

    def around(ref, row, count):
        return [three(ref, row + d) for d in range(-1, count + 1)]

    def coarse(states, row, count):
        return steps(
            states,
            [rows_of(rhw, row + d, 0) for d in range(-1, count + 1)],
            [rows_of(rhw, row + d, 1) for d in range(count)],
            [turning(row + d, brick * m, 2.0, all_rows, COARSE_TIME) for d in range(count)],
            COARSE_TIME,
            2,
            [(rows_of(rhw, row + d, 2), rows_of(rhw, row + d, 3)) for d in range(count)],
        )

    def store(ref, row, new):
        for d, rows in enumerate(new):
            put_three(ref, row + d, rows)

    loop(1, n - 1, n - 2, lambda row, c: store(s1, row, fine(around(ini, row, c), row, c)))
    loop(2, n - 2, n - 4, lambda row, c: store(s2, row, fine(around(s1, row, c), row, c)))

    @pl.when(lane == 0)
    def _():
        def copied(row, count):
            for d in range(count):
                emit(tiles, (), nj, row + d, three(s2, row + d))

        loop(2, n - 2, 4, copied)

    @pl.when(lane != 0)
    def _():
        def restrict(row, count):
            for d in range(count):
                low, high = 2 * (row + d), 2 * (row + d) + 1
                put_three(rc, row + d, average3(three(ini, low), three(ini, high)))

        def restrict_depth(row, count):
            for d in range(count):
                low, high = 2 * (row + d), 2 * (row + d) + 1
                deep = average(rows_of(hw, low, 0), rows_of(hw, high, 0))
                dry = average(rows_of(hw, low, 1), rows_of(hw, high, 1))
                for k, x in enumerate((deep, dry, *sideways(deep, 2))):
                    put(rhw, (row + d, k), x)

        loop(0, m, 4, restrict)
        loop(0, m, 4, restrict_depth)
        loop(1, m - 1, m - 2, lambda row, c: store(c1, row, coarse(around(rc, row, c), row, c)))

        def again(row, count):
            for d in range(count):
                low, high = 2 * (row + d), 2 * (row + d) + 1
                put_three(rf, row + d, average3(three(s2, low), three(s2, high)))

        loop(1, m - 1, m - 2, again)

        def correct(row, count):
            both = [interleave(a, b) for a, b in zip(around(rf, row, count), around(c1, row, count))]
            store(dif, row, [difference(z) for z in coarse(both, row, count)])

        loop(2, m - 2, m - 4, correct)

        def prolonged(half, count):
            pairs = around(c1, half, count)
            twice = [pairs[(d + 1) // 2] for d in range(2 * count + 2)]
            store(p1, 2 * half, fine(twice, 2 * half, 2 * count))

        loop(2, m - 2, m - 4, prolonged)
        for row in (3, n - 4):
            store(p1, row, fine([three(c1, (row + d) // 2) for d in (-1, 0, 1)], row, 1))

        def last(row, count):
            for d, rows in enumerate(fine(around(p1, row, count), row, count)):
                emit(tiles, (), nj, row + d, added(rows, three(dif, (row + d) // 2)))

        loop(4, n - 4, n - 8, last)


def edge_kernel(nj, bricks, n, turned, near, ini, hw, s1, rc, rhw, rf, c1, p1, *refs):
    lane = lax.axis_index("cuts")
    brick = lax.axis_index("brick")
    all_rows = n * bricks
    m = n // 2
    wide = nj * SUB
    if turned:
        ready, _, out, tiles, sems = refs
    else:
        middle, out, tiles, sems = refs

    def own(s, i, count):
        return i if s == 0 else count - 1 - i

    def depth(s, i):
        return rows_of(near, (-1 - i) * PER + 3) if i < 0 else rows_of(hw, own(s, i, n), 0)

    def wet(s, i):
        return rows_of(near, (-1 - i) * PER + 4) if i < 0 else rows_of(hw, own(s, i, n), 1)

    def initial(s, i):
        if i < 0:
            return tuple(rows_of(near, (-1 - i) * PER + k) for k in range(3))
        return three(ini, own(s, i, n))

    def known(ref, s, ids):
        return {i: three(ref, own(s, i, ref.shape[0])) for i in ids}

    def inside(s):
        there = brick > 0 if s == 0 else brick < bricks - 1
        return jnp.where(there, 1.0, 0.0).astype(jnp.float32)

    def advance(s, ids, state, heights, wets, turn, dt, cols, beside):
        run = list(ids) if s == 0 else list(ids)[::-1]
        way = 1 if s == 0 else -1
        span = [run[0] - way, *run, run[-1] + way]
        sides = [beside(i) for i in run]
        new = steps([state(i) for i in span], [heights(i) for i in span], [wets(i) for i in run], [turn(i) for i in run], dt, cols, sides)
        return {i: masked(x, inside(s)) if i < 0 else x for i, x in zip(run, new)}

    def fine(s, ids, state, beside):
        turn = lambda i: turning(jnp.int32(own(s, i, n)), brick * n, 1.0, all_rows, FINE_TIME)
        return advance(s, ids, state, lambda i: depth(s, i), lambda i: wet(s, i), turn, FINE_TIME, 1, beside)

    def coarse(s, ids, state, deep, dry, beside):
        turn = lambda i: turning(jnp.int32(own(s, i, m)), brick * m, 2.0, all_rows, COARSE_TIME)
        return advance(s, ids, state, deep.__getitem__, dry.__getitem__, turn, COARSE_TIME, 2, beside.__getitem__)

    def sides_from(s, outer):
        held = {i: sideways(depth(s, i), 1) for i in range(outer, 0)}
        return lambda i: held[i] if i < 0 else (rows_of(hw, own(s, i, n), 2), rows_of(hw, own(s, i, n), 3))

    def flown(s, outer, beside):
        start = {i: initial(s, i) for i in range(outer - 2, 2)}
        one = fine(s, range(outer - 1, 1), start.__getitem__, beside)
        one.update(known(s1, s, (1, 2)))
        return fine(s, range(outer, 2), one.__getitem__, beside)

    def sent(ref, s, count, sem):
        at = 0 if s == 0 else SUB - count
        where = 0 if s == 0 else (n // SUB - 1) * wide
        src = ref.reshape(3, wide, SUB, LANES).at[:, :, at : at + count, :]
        return pltpu.make_async_copy(src, out.at[:, where : where + wide, at : at + count, :], sems.at[sem])

    def earlier(s, count):
        return sent(ready, 1 - s, count, 0) if turned else pltpu.make_async_copy(middle, out, sems.at[0])

    def finished(s, count, rows_of_side):
        for i, x in rows_of_side().items():
            if i >= 0:
                emit(tiles, (), nj, own(s, i, SUB), x)
        if turned:
            later = sent(tiles, s, count, 1)
            later.start()
            later.wait()
        earlier(s, count).wait()

    def first_end(s):
        return flown(s, 0, sides_from(s, -1))

    def second_end(s):
        beside = sides_from(s, -3)
        two = flown(s, -2, beside)
        fresh = {i: average3(two[2 * i], two[2 * i + 1]) for i in (-1, 0)}
        fresh.update(known(rf, s, (1, 2)))
        start = {i: average3(initial(s, 2 * i), initial(s, 2 * i + 1)) for i in (-2, -1)}
        start.update(known(rc, s, (0, 1)))
        deep = {i: average(depth(s, 2 * i), depth(s, 2 * i + 1)) for i in (-2, -1)}
        deep.update({i: rows_of(rhw, own(s, i, m), 0) for i in (0, 1, 2)})
        dry = {-1: average(wet(s, -2), wet(s, -1))}
        dry.update({i: rows_of(rhw, own(s, i, m), 1) for i in (0, 1)})
        aside = {-1: sideways(deep[-1], 2)}
        aside.update({i: (rows_of(rhw, own(s, i, m), 2), rows_of(rhw, own(s, i, m), 3)) for i in (0, 1)})
        first = coarse(s, (-1, 0), start.__getitem__, deep, dry, aside)
        first.update(known(c1, s, (1, 2)))
        both = {i: interleave(fresh[i], first[i]) for i in range(-1, 3)}
        add = {i: difference(z) for i, z in coarse(s, (0, 1), both.__getitem__, deep, dry, aside).items()}
        one = fine(s, range(-1, 3), lambda i: first[i // 2], beside)
        one.update(known(p1, s, (3, 4)))
        return {i: added(x, add[i // 2]) for i, x in fine(s, range(4), one.__getitem__, beside).items()}

    one, two = int(turned), 1 - int(turned)
    pl.when(lane == 0)(lambda: earlier(one, 2).start())
    pl.when(lane != 0)(lambda: earlier(two, 4).start())
    pl.when(lane == 0)(lambda: finished(one, 2, lambda: first_end(one)))
    pl.when(lane != 0)(lambda: finished(two, 4, lambda: second_end(two)))


def tiled(a):
    *lead, rows, cols = a.shape
    a = a.reshape(*lead, rows // SUB, SUB, cols // LANES, LANES)
    return jnp.swapaxes(a, -3, -2).reshape(*lead, rows * cols // LANES, LANES)


def untiled(a, rows, cols):
    lead = a.shape[:-2]
    a = a.reshape(*lead, rows // SUB, cols // LANES, SUB, LANES)
    return jnp.swapaxes(a, -3, -2).reshape(*lead, rows, cols)


def shards(initial, depth, mask):
    bricks = lax.axis_size("brick")
    n, cols = depth.shape
    nj = cols // (SUB * LANES)
    row = (nj, SUB, LANES)
    f32 = jnp.float32
    initial, depth, mask = tiled(initial), tiled(depth), tiled(mask)
    tile = nj * SUB * SUB
    size = depth.shape[0]
    params = pltpu.CompilerParams(vmem_limit_bytes=VMEM_LIMIT)
    far = pl.BlockSpec(memory_space=pltpu.HBM)
    local = pl.BlockSpec(memory_space=pltpu.VMEM)

    def hold(rows, count):
        return jax.ShapeDtypeStruct((rows, count, *row), f32)

    def rows8(a):
        return a.reshape(*a.shape[:-2], -1, SUB, LANES)

    wide = nj * SUB
    packed = pl.pallas_call(
        functools.partial(pack_kernel, nj),
        out_shape=jax.ShapeDtypeStruct((PACKED, *row), f32),
        in_specs=[far] * 3,
        out_specs=local,
        scratch_shapes=[
            pltpu.VMEM((3, wide, HALO, LANES), f32),
            pltpu.VMEM((wide, HALO, LANES), f32),
            pltpu.VMEM((wide, HALO, LANES), jnp.int32),
            pltpu.SemaphoreType.DMA((3,)),
        ],
        compiler_params=params,
        name="pack",
    )(*(pltpu.with_memory_space_constraint(rows8(a), pltpu.HBM) for a in (initial, depth, mask)))
    packed, initial, depth, mask = lax.optimization_barrier((packed, initial, depth, mask))

    up = [(2 * i + 1, 2 * i + 2) for i in range(bricks - 1)]
    near = lax.ppermute(packed, ("brick", "cuts"), up + [(b, a) for a, b in up])

    inner, *held = pl.pallas_call(
        functools.partial(middle_kernel, nj, bricks),
        out_shape=[
            jax.ShapeDtypeStruct((3, size, LANES), f32),
            hold(n, 3),
            hold(n, 4),
            hold(n, 3),
            hold(n // 2, 3),
            hold(n // 2, 4),
            hold(n // 2, 3),
            hold(n // 2, 3),
            hold(n, 3),
        ],
        in_specs=[local] * 3,
        out_specs=[local] * 9,
        scratch_shapes=[
            pltpu.VMEM((n, 3, *row), f32),
            pltpu.VMEM((n // 2, 3, *row), f32),
        ],
        compiler_params=params,
        cost_estimate=pl.CostEstimate(flops=60 * 5 * n * cols, bytes_accessed=10 * n * cols * 4, transcendentals=0),
        name="middle",
    )(initial, depth, mask)

    def edges(turned, near, *more):
        result = jax.ShapeDtypeStruct((3, size // SUB, SUB, LANES), f32)
        part = jax.ShapeDtypeStruct((3, tile, LANES), f32)
        return pl.pallas_call(
            functools.partial(edge_kernel, nj, bricks, n, turned),
            out_shape=result if turned else [result, part],
            in_specs=[local] * 10 + ([far] if turned else []),
            out_specs=far if turned else [far, local],
            scratch_shapes=[pltpu.VMEM(part.shape, f32)] * turned + [pltpu.SemaphoreType.DMA((2,))],
            input_output_aliases={10: 0} if turned else {},
            compiler_params=params,
            cost_estimate=pl.CostEstimate(flops=60 * n * cols, bytes_accessed=n * cols * 4, transcendentals=0),
            name="edges",
        )(near, *held, *more)

    near, inner, *held = lax.optimization_barrier((near, inner, *held))
    other = lax.ppermute(near, "cuts", [(0, 1), (1, 0)])
    whole, ready = edges(False, near, rows8(inner))
    whole = edges(True, other, ready, whole)
    return untiled(whole.reshape(3, size, LANES), n, cols)[None]


def solution(mesh):
    placed = (P(None, ("grp", "brick"), None), P("brick", None), P("brick", None))
    return jax.shard_map(
        shards,
        mesh=mesh,
        in_specs=placed,
        out_specs=P("cuts", None, ("grp", "brick"), None),
        check_vma=False,
    )
```

time: 22.5 us -> 18.8 us (0.84); the launches traced: 22.4 us -> 18.4 us
  Pallas kernels: 17.7 us -> 13.2 us
  waiting for transfers between devices: 0.01 us -> 0.59 us
    pallas_call x1, Pallas kernels: 12 us -> 8.57 us  [shards(): pl.pallas_call(functools.partial(middle_kernel, nj, bricks), out_shape=[j...]
    pallas_call x2, Pallas kernels: 4.28 us -> 3.38 us  [edges(): pl.pallas_call(functools.partial(edge_kernel, nj, bricks, n, turned), out...]
    ppermute x1, waiting for transfers between devices: 0.01 us -> 0.38 us  [shards(): other = lax.ppermute(near, 'cuts', [(0, 1), (1, 0)])]
  transfers between devices with their start and end apart: 2 -> 2, of which waited for: 0 -> 2; matrix products, arithmetic and copies ran while one was open for 0% -> 0% of each run, Pallas kernels for 63% -> 54%
where the time goes in v2:
time: 18.8 us; the launch traced here: 18.4 us
  Pallas kernels  13.2 us (70%)
  starting transfers between devices  4.54 us (24%)
  waiting for transfers between devices  0.59 us (3%)
    pallas_call x1, Pallas kernels, shards(): pl.pallas_call(functools.partial(middle_kernel, nj, bricks), out_shape=[j...  8.57 us
    ppermute x1, starting transfers between devices, shards(): near = lax.ppermute(packed, ('brick', 'cuts'), up + [(b, a) for a, b in up])  4.53 us
    pallas_call x2, Pallas kernels, edges(): pl.pallas_call(functools.partial(edge_kernel, nj, bricks, n, turned), out...  3.38 us
    pallas_call x1, Pallas kernels, shards(): pl.pallas_call(functools.partial(pack_kernel, nj), out_shape=jax.ShapeDty...  1.28 us
  transfers between devices with their start and end apart: 2, of which 2 were waited for; matrix products, arithmetic and copies ran while one was open for 0% of the time, Pallas kernels for 54%

profile of v2, /device:TPU:1, one launch (start us, length us, event | category | flops | bytes accessed | tf_op | source)
XLA Modules:
  0.0 18.4 jit_solution(10422253946538700729)
XLA Ops:
  0.0 0.0 copy-start
  0.0 0.0 copy-start.1
  0.0 0.0 copy-start.2
  0.0 1.3 %pack.1 = f32[19,5,8,128]{3,2,1,0:T(8,128)S(1)} custom-call(f32[3,160,8,128]{3,2,1,0:T(8,128)} %bitcast.27, f32[160,8,128]{2,1,0:T(8,128)} %bitcast.29, s32[160,8,128]{2,1,0:T(8,128)} %bitcast.31), custom_call_target="tpu_custom_call" | custom-call | tf_op jit(solution)/shard_map/pack/pallas_call | solution.py:450
  1.3 4.5 %collective-permute-start = (f32[19,5,8,128]{3,2,1,0:T(8,128)S(1)}, f32[19,5,8,128]{3,2,1,0:T(8,128)S(1)}, u32[]{:S(2)}, u32[]{:S(2)}) collective-permute-start(f32[19,5,8,128]{3,2,1,0:T(8,128)S(1)} %pack.1), channel_id=1, source_target_pairs={{1,2},{3,4},{5,6},{7,8},{9,10},{11,12},{13,14},{2,1},{4,3},{6,5},{... | collective-permute-start | bytes 1167368 | tf_op jit(solution)/shard_map/ppermute | solution.py:467
  5.8 0.0 copy-done
  5.8 0.0 copy-done.1
  5.9 0.0 copy-done.2
  5.9 8.6 %middle.1 = (f32[3,1280,128]{2,1,0:T(8,128)S(1)}, f32[32,3,5,8,128]{4,3,2,1,0:T(8,128)S(1)}, f32[32,4,5,8,128]{4,3,2,1,0:T(8,128)S(1)}, f32[32,3,5,8,128]{4,3,2,...) custom-call(f32[3,1280,128]{2,1,0:T(8,128)S(1)} %bitcast.28, ...), custom_call_target="tpu_custom_call" | custom-call | flops 49152000 | bytes 6553600 | tf_op jit(solution)/shard_map/middle/pallas_call | solution.py:469
  14.4 0.2 %collective-permute-done.near = f32[19,5,8,128]{3,2,1,0:T(8,128)S(1)} collective-permute-done((f32[19,5,8,128]{3,2,1,0:T(8,128)S(1)}, f32[19,5,8,128]{3,2,1,0:T(8,128)S(1)}, u32[]{:S(2)}, u32[]{:S(2)}) %collective-permute-start) | collective-permute-done | bytes 389152 | tf_op jit(solution)/shard_map/ppermute | solution.py:467
  14.7 0.0 collective-permute-start.1
  14.7 1.3 %edges.2 = (f32[3,160,8,128]{3,2,1,0:T(8,128)}, f32[3,320,128]{2,1,0:T(8,128)S(1)}) custom-call(f32[19,5,8,128]{3,2,1,0:T(8,128)S(1)} %collective-permute-done.near, f32[32,3,5,8,128]{4,3,2,1,0:T(8,128)S(1)} %get-tuple-element.44.ini, f32[32,4,5,8,128]{4,3,2,1,0:T(8,128)S(1)} %get-tuple-element.45.hw, f32[32,3,5,8,128]{4,3,2,1,0:T(8,128)S(1)} %get-tuple-element.46.s1, ...), custom_call_target="tpu_custom_call" | custom-call | flops 9830400 | bytes 655360 | tf_op jit(solution)/shard_map/edges/pallas_call | solution.py:496
  16.0 0.4 %collective-permute-done.1.near = f32[19,5,8,128]{3,2,1,0:T(8,128)S(1)} collective-permute-done((f32[19,5,8,128]{3,2,1,0:T(8,128)S(1)}, f32[19,5,8,128]{3,2,1,0:T(8,128)S(1)}, u32[]{:S(2)}, u32[]{:S(2)}) %collective-permute-start.1) | collective-permute-done | bytes 389152 | tf_op jit(solution)/shard_map/ppermute | solution.py:509
  16.4 2.1 %edges.3 = f32[3,160,8,128]{3,2,1,0:T(8,128)} custom-call(f32[19,5,8,128]{3,2,1,0:T(8,128)S(1)} %collective-permute-done.1.near, f32[32,3,5,8,128]{4,3,2,1,0:T(8,128)S(1)} %get-tuple-element.44.ini, f32[32,4,5,8,128]{4,3,2,1,0:T(8,128)S(1)} %get-tuple-element.45.hw, f32[32,3,5,8,128]{4,3,2,1,0:T(8,128)S(1)} %get-tuple-element.46.s1, ...), custom_call_target="tpu_custom_call", output_to_operand_aliasing={{}: (10, {})} | custom-call | flops 9830400 | bytes 655360 | tf_op jit(solution)/shard_map/edges/pallas_call | solution.py:496
Async XLA Ops:
  0.0 5.8 %copy-start = (f32[3,32,5120]{2,1,0:T(8,128)S(1)}, f32[3,32,5120]{2,1,0:T(8,128)}, u32[]{:S(2)}) copy-start(f32[3,32,5120]{2,1,0:T(8,128)} %param.3) | copy-start | bytes 5898244
  0.0 5.8 %copy-start.1 = (f32[32,5120]{1,0:T(8,128)S(1)}, f32[32,5120]{1,0:T(8,128)}, u32[]{:S(2)}) copy-start(f32[32,5120]{1,0:T(8,128)} %param.4) | copy-start | bytes 1966084
  0.0 5.9 %copy-start.2 = (s32[32,5120]{1,0:T(8,128)S(1)}, s32[32,5120]{1,0:T(8,128)}, u32[]{:S(2)}) copy-start(s32[32,5120]{1,0:T(8,128)} %param.5) | copy-start | bytes 1966084
  1.3 13.4 %collective-permute-start = (f32[19,5,8,128]{3,2,1,0:T(8,128)S(1)}, f32[19,5,8,128]{3,2,1,0:T(8,128)S(1)}, u32[]{:S(2)}, u32[]{:S(2)}) collective-permute-start(f32[19,5,8,128]{3,2,1,0:T(8,128)S(1)} %pack.1), channel_id=1, source_target_pairs={{1,2},{3,4},{5,6},{7,8},{9,10},{11,12},{13,14},{2,1},{4,3},{6,5},{... | collective-permute-start | bytes 1167368 | tf_op jit(solution)/shard_map/ppermute | solution.py:467
  14.7 1.7 %collective-permute-start.1 = (f32[19,5,8,128]{3,2,1,0:T(8,128)S(1)}, f32[19,5,8,128]{3,2,1,0:T(8,128)S(1)}, u32[]{:S(2)}, u32[]{:S(2)}) collective-permute-start(f32[19,5,8,128]{3,2,1,0:T(8,128)S(1)} %collective-permute-done.near), channel_id=1, source_target_pairs={{0,1},{1,0},{2,3},{3,2},{4,5},{5,4},{6,7},{7,6},{8,9},{9,8},{10,11... | collective-permute-start | bytes 1167368 | tf_op jit(solution)/shard_map/ppermute | solution.py:509

commit v3 on v2

--- a/solution.py
+++ b/solution.py
@@ -79,6 +79,14 @@
     return each(one, low, high)
 
 
+def average_even(low, high):
+    def one(a, b):
+        s = a + b
+        return (s + pltpu.roll(s, LANES - 1, 1)) * 0.25
+
+    return tuple(each(one, a, b) for a, b in zip(low, high))
+
+
 def average3(low, high):
     return tuple(average(a, b) for a, b in zip(low, high))
 
@@ -173,21 +181,6 @@
     pl.when(lane != 0)(lambda: fill(depth.shape[0] - wide, SUB - HALO, lambda d: HALO - 1 - d))
 
 
-def loop(low, high, count, body):
-    times, rest = divmod(high - low, count)
-
-    def run(i, carry):
-        body(low + i * count, count)
-        return carry
-
-    if times > 1:
-        lax.fori_loop(0, times, run, 0)
-    elif times:
-        body(low, count)
-    if rest:
-        body(high - rest, rest)
-
-
 def sideways(h, cols):
     lane = lane_ids()
     return next_col(h, cols, lane >= LANES - cols), prev_col(h, cols, lane < cols)
@@ -202,7 +195,7 @@
     tile = nj * SUB * SUB
     parts = n // SUB
 
-    def load(t, carry):
+    def load(t):
         for r in range(SUB):
             row = t * SUB + r
             high = []
@@ -215,9 +208,9 @@
             put(hw, (row, 0), high)
             for k, side in enumerate(sideways(high, 1)):
                 put(hw, (row, 2 + k), side)
-        return carry
-
-    lax.fori_loop(0, parts, load, 0)
+
+    for t in range(parts):
+        load(t)
 
     def fine(states, row, count):
         return steps(
@@ -248,8 +241,8 @@
         for d, rows in enumerate(new):
             put_three(ref, row + d, rows)
 
-    loop(1, n - 1, n - 2, lambda row, c: store(s1, row, fine(around(ini, row, c), row, c)))
-    loop(2, n - 2, n - 4, lambda row, c: store(s2, row, fine(around(s1, row, c), row, c)))
+    store(s1, 1, fine(around(ini, 1, n - 2), 1, n - 2))
+    store(s2, 2, fine(around(s1, 2, n - 4), 2, n - 4))
 
     @pl.when(lane == 0)
     def _():
@@ -257,7 +250,7 @@
             for d in range(count):
                 emit(tiles, (), nj, row + d, three(s2, row + d))
 
-        loop(2, n - 2, 4, copied)
+        copied(2, n - 4)
 
     @pl.when(lane != 0)
     def _():
@@ -274,29 +267,29 @@
                 for k, x in enumerate((deep, dry, *sideways(deep, 2))):
                     put(rhw, (row + d, k), x)
 
-        loop(0, m, 4, restrict)
-        loop(0, m, 4, restrict_depth)
-        loop(1, m - 1, m - 2, lambda row, c: store(c1, row, coarse(around(rc, row, c), row, c)))
+        restrict(0, m)
+        restrict_depth(0, m)
+        store(c1, 1, coarse(around(rc, 1, m - 2), 1, m - 2))
 
         def again(row, count):
             for d in range(count):
                 low, high = 2 * (row + d), 2 * (row + d) + 1
-                put_three(rf, row + d, average3(three(s2, low), three(s2, high)))
-
-        loop(1, m - 1, m - 2, again)
+                put_three(rf, row + d, average_even(three(s2, low), three(s2, high)))
+
+        again(1, m - 2)
 
         def correct(row, count):
             both = [interleave(a, b) for a, b in zip(around(rf, row, count), around(c1, row, count))]
             store(dif, row, [difference(z) for z in coarse(both, row, count)])
 
-        loop(2, m - 2, m - 4, correct)
+        correct(2, m - 4)
 
         def prolonged(half, count):
             pairs = around(c1, half, count)
             twice = [pairs[(d + 1) // 2] for d in range(2 * count + 2)]
             store(p1, 2 * half, fine(twice, 2 * half, 2 * count))
 
-        loop(2, m - 2, m - 4, prolonged)
+        prolonged(2, m - 4)
         for row in (3, n - 4):
             store(p1, row, fine([three(c1, (row + d) // 2) for d in (-1, 0, 1)], row, 1))
 
@@ -304,7 +297,7 @@
             for d, rows in enumerate(fine(around(p1, row, count), row, count)):
                 emit(tiles, (), nj, row + d, added(rows, three(dif, (row + d) // 2)))
 
-        loop(4, n - 4, n - 8, last)
+        last(4, n - 8)
 
 
 def edge_kernel(nj, bricks, n, turned, near, ini, hw, s1, rc, rhw, rf, c1, p1, *refs):
@@ -389,9 +382,6 @@
 
     def second_end(s):
         beside = sides_from(s, -3)
-        two = flown(s, -2, beside)
-        fresh = {i: average3(two[2 * i], two[2 * i + 1]) for i in (-1, 0)}
-        fresh.update(known(rf, s, (1, 2)))
         start = {i: average3(initial(s, 2 * i), initial(s, 2 * i + 1)) for i in (-2, -1)}
         start.update(known(rc, s, (0, 1)))
         deep = {i: average(depth(s, 2 * i), depth(s, 2 * i + 1)) for i in (-2, -1)}
@@ -402,11 +392,15 @@
         aside.update({i: (rows_of(rhw, own(s, i, m), 2), rows_of(rhw, own(s, i, m), 3)) for i in (0, 1)})
         first = coarse(s, (-1, 0), start.__getitem__, deep, dry, aside)
         first.update(known(c1, s, (1, 2)))
+        one = fine(s, range(-1, 3), lambda i: first[i // 2], beside)
+        one.update(known(p1, s, (3, 4)))
+        last = fine(s, range(4), one.__getitem__, beside)
+        two = flown(s, -2, beside)
+        fresh = {i: average_even(two[2 * i], two[2 * i + 1]) for i in (-1, 0)}
+        fresh.update(known(rf, s, (1, 2)))
         both = {i: interleave(fresh[i], first[i]) for i in range(-1, 3)}
         add = {i: difference(z) for i, z in coarse(s, (0, 1), both.__getitem__, deep, dry, aside).items()}
-        one = fine(s, range(-1, 3), lambda i: first[i // 2], beside)
-        one.update(known(p1, s, (3, 4)))
-        return {i: added(x, add[i // 2]) for i, x in fine(s, range(4), one.__getitem__, beside).items()}
+        return {i: added(x, add[i // 2]) for i, x in last.items()}
 
     one, two = int(turned), 1 - int(turned)
     pl.when(lane == 0)(lambda: earlier(one, 2).start())

time: 18.8 us -> 18.7 us (level)
  Pallas kernels: 13.2 us -> 12.7 us
  waiting for transfers between devices: 0.59 us -> 1.06 us
    pallas_call x1, Pallas kernels: 8.57 us -> 8.14 us  [shards(): pl.pallas_call(functools.partial(middle_kernel, nj, bricks), out_shape=[j...]
    ppermute x1, waiting for transfers between devices: 0.22 us -> 0.64 us  [shards(): near = lax.ppermute(packed, ('brick', 'cuts'), up + [(b, a) for a, b in up])]
  transfers between devices with their start and end apart: 2 -> 2, of which waited for: 2 -> 2; matrix products, arithmetic and copies ran while one was open for 0% -> 0% of each run, Pallas kernels for 54% -> 51%
where the time goes in v3:
time: 18.7 us; the launch traced here: 18.4 us
  Pallas kernels  12.7 us (68%)
  starting transfers between devices  4.54 us (24%)
  waiting for transfers between devices  1.06 us (6%)
    pallas_call x1, Pallas kernels, shards(): pl.pallas_call(functools.partial(middle_kernel, nj, bricks), out_shape=[j...  8.14 us
    ppermute x1, starting transfers between devices, shards(): near = lax.ppermute(packed, ('brick', 'cuts'), up + [(b, a) for a, b in up])  4.53 us
    pallas_call x2, Pallas kernels, edges(): pl.pallas_call(functools.partial(edge_kernel, nj, bricks, n, turned), out...  3.3 us
    pallas_call x1, Pallas kernels, shards(): pl.pallas_call(functools.partial(pack_kernel, nj), out_shape=jax.ShapeDty...  1.28 us
    ppermute x1, waiting for transfers between devices, shards(): near = lax.ppermute(packed, ('brick', 'cuts'), up + [(b, a) for a, b in up])  0.64 us
    ppermute x1, waiting for transfers between devices, shards(): other = lax.ppermute(near, 'cuts', [(0, 1), (1, 0)])  0.42 us
  transfers between devices with their start and end apart: 2, of which 2 were waited for; matrix products, arithmetic and copies ran while one was open for 0% of the time, Pallas kernels for 51%

profile of v3, /device:TPU:1, one launch (start us, length us, event | category | flops | bytes accessed | tf_op | source)
XLA Modules:
  0.0 18.4 jit_solution(4718688348952552385)
XLA Ops:
  0.0 0.0 copy-start
  0.0 0.0 copy-start.1
  0.0 0.0 copy-start.2
  0.0 1.3 %pack.1 = f32[19,5,8,128]{3,2,1,0:T(8,128)S(1)} custom-call(f32[3,160,8,128]{3,2,1,0:T(8,128)} %bitcast.27, f32[160,8,128]{2,1,0:T(8,128)} %bitcast.29, s32[160,8,128]{2,1,0:T(8,128)} %bitcast.31), custom_call_target="tpu_custom_call" | custom-call | tf_op jit(solution)/shard_map/pack/pallas_call | solution.py:444
  1.3 4.5 %collective-permute-start = (f32[19,5,8,128]{3,2,1,0:T(8,128)S(1)}, f32[19,5,8,128]{3,2,1,0:T(8,128)S(1)}, u32[]{:S(2)}, u32[]{:S(2)}) collective-permute-start(f32[19,5,8,128]{3,2,1,0:T(8,128)S(1)} %pack.1), channel_id=1, source_target_pairs={{1,2},{3,4},{5,6},{7,8},{9,10},{11,12},{13,14},{2,1},{4,3},{6,5},{... | collective-permute-start | bytes 1167368 | tf_op jit(solution)/shard_map/ppermute | solution.py:461
  5.8 0.0 copy-done
  5.8 0.0 copy-done.1
  5.9 0.0 copy-done.2
  5.9 8.1 %middle.1 = (f32[3,1280,128]{2,1,0:T(8,128)S(1)}, f32[32,3,5,8,128]{4,3,2,1,0:T(8,128)S(1)}, f32[32,4,5,8,128]{4,3,2,1,0:T(8,128)S(1)}, f32[32,3,5,8,128]{4,3,2,...) custom-call(f32[3,1280,128]{2,1,0:T(8,128)S(1)} %bitcast.28, ...), custom_call_target="tpu_custom_call" | custom-call | flops 49152000 | bytes 6553600 | tf_op jit(solution)/shard_map/middle/pallas_call | solution.py:463
  14.0 0.6 %collective-permute-done.near = f32[19,5,8,128]{3,2,1,0:T(8,128)S(1)} collective-permute-done((f32[19,5,8,128]{3,2,1,0:T(8,128)S(1)}, f32[19,5,8,128]{3,2,1,0:T(8,128)S(1)}, u32[]{:S(2)}, u32[]{:S(2)}) %collective-permute-start) | collective-permute-done | bytes 389152 | tf_op jit(solution)/shard_map/ppermute | solution.py:461
  14.7 0.0 collective-permute-start.1
  14.7 1.3 %edges.2 = (f32[3,160,8,128]{3,2,1,0:T(8,128)}, f32[3,320,128]{2,1,0:T(8,128)S(1)}) custom-call(f32[19,5,8,128]{3,2,1,0:T(8,128)S(1)} %collective-permute-done.near, f32[32,3,5,8,128]{4,3,2,1,0:T(8,128)S(1)} %get-tuple-element.44.ini, f32[32,4,5,8,128]{4,3,2,1,0:T(8,128)S(1)} %get-tuple-element.45.hw, f32[32,3,5,8,128]{4,3,2,1,0:T(8,128)S(1)} %get-tuple-element.46.s1, ...), custom_call_target="tpu_custom_call" | custom-call | flops 9830400 | bytes 655360 | tf_op jit(solution)/shard_map/edges/pallas_call | solution.py:490
  16.0 0.4 %collective-permute-done.1.near = f32[19,5,8,128]{3,2,1,0:T(8,128)S(1)} collective-permute-done((f32[19,5,8,128]{3,2,1,0:T(8,128)S(1)}, f32[19,5,8,128]{3,2,1,0:T(8,128)S(1)}, u32[]{:S(2)}, u32[]{:S(2)}) %collective-permute-start.1) | collective-permute-done | bytes 389152 | tf_op jit(solution)/shard_map/ppermute | solution.py:503
  16.4 2.0 %edges.3 = f32[3,160,8,128]{3,2,1,0:T(8,128)} custom-call(f32[19,5,8,128]{3,2,1,0:T(8,128)S(1)} %collective-permute-done.1.near, f32[32,3,5,8,128]{4,3,2,1,0:T(8,128)S(1)} %get-tuple-element.44.ini, f32[32,4,5,8,128]{4,3,2,1,0:T(8,128)S(1)} %get-tuple-element.45.hw, f32[32,3,5,8,128]{4,3,2,1,0:T(8,128)S(1)} %get-tuple-element.46.s1, ...), custom_call_target="tpu_custom_call", output_to_operand_aliasing={{}: (10, {})} | custom-call | flops 9830400 | bytes 655360 | tf_op jit(solution)/shard_map/edges/pallas_call | solution.py:490
Async XLA Ops:
  0.0 5.8 %copy-start = (f32[3,32,5120]{2,1,0:T(8,128)S(1)}, f32[3,32,5120]{2,1,0:T(8,128)}, u32[]{:S(2)}) copy-start(f32[3,32,5120]{2,1,0:T(8,128)} %param.3) | copy-start | bytes 5898244
  0.0 5.8 %copy-start.1 = (f32[32,5120]{1,0:T(8,128)S(1)}, f32[32,5120]{1,0:T(8,128)}, u32[]{:S(2)}) copy-start(f32[32,5120]{1,0:T(8,128)} %param.4) | copy-start | bytes 1966084
  0.0 5.9 %copy-start.2 = (s32[32,5120]{1,0:T(8,128)S(1)}, s32[32,5120]{1,0:T(8,128)}, u32[]{:S(2)}) copy-start(s32[32,5120]{1,0:T(8,128)} %param.5) | copy-start | bytes 1966084
  1.3 13.4 %collective-permute-start = (f32[19,5,8,128]{3,2,1,0:T(8,128)S(1)}, f32[19,5,8,128]{3,2,1,0:T(8,128)S(1)}, u32[]{:S(2)}, u32[]{:S(2)}) collective-permute-start(f32[19,5,8,128]{3,2,1,0:T(8,128)S(1)} %pack.1), channel_id=1, source_target_pairs={{1,2},{3,4},{5,6},{7,8},{9,10},{11,12},{13,14},{2,1},{4,3},{6,5},{... | collective-permute-start | bytes 1167368 | tf_op jit(solution)/shard_map/ppermute | solution.py:461
  14.7 1.7 %collective-permute-start.1 = (f32[19,5,8,128]{3,2,1,0:T(8,128)S(1)}, f32[19,5,8,128]{3,2,1,0:T(8,128)S(1)}, u32[]{:S(2)}, u32[]{:S(2)}) collective-permute-start(f32[19,5,8,128]{3,2,1,0:T(8,128)S(1)} %collective-permute-done.near), channel_id=1, source_target_pairs={{0,1},{1,0},{2,3},{3,2},{4,5},{5,4},{6,7},{7,6},{8,9},{9,8},{10,11... | collective-permute-start | bytes 1167368 | tf_op jit(solution)/shard_map/ppermute | solution.py:503

commit v4 on v3

--- a/solution.py
+++ b/solution.py
@@ -158,24 +158,17 @@
 
     def fill(tile, at, row_of):
         there = pl.ds(tile, wide), pl.ds(at, HALO)
-        copies = [
-            pltpu.make_async_copy(initial.at[:, *there, :], initial_v, sems.at[0]),
-            pltpu.make_async_copy(depth.at[*there, :], depth_v, sems.at[1]),
-            pltpu.make_async_copy(mask.at[*there, :], mask_v, sems.at[2]),
-        ]
+        parts = [(depth, depth_v), (mask, mask_v)] + [(initial.at[k], initial_v.at[k]) for k in range(3)]
+        copies = [pltpu.make_async_copy(src.at[*there, :], dst, sems.at[i]) for i, (src, dst) in enumerate(parts)]
         for copy in copies:
             copy.start()
-        for copy in copies:
+        forms = [lambda a: a * 4.0, wetness] + [lambda a, k=k: a * SCALE[k] for k in range(3)]
+        for place, copy, (_, ref), form in zip((3, 4, 0, 1, 2), copies, parts, forms):
             copy.wait()
-        flat = [ref.reshape(*ref.shape[:-3], wide * HALO, LANES) for ref in (initial_v, depth_v, mask_v)]
-        for d in range(HALO):
-            for j in range(nj):
-                at = pl.ds(row_of(d) + j * HALO, SUB, stride=nj * HALO)
-                for k in range(3):
-                    out[d * PER + k, j] = flat[0][k, at, :] * SCALE[k]
-                out[d * PER + 3, j] = flat[1][at, :] * 4.0
-                if d < HALO - 1:
-                    out[d * PER + 4, j] = wetness(flat[2][at, :])
+            flat = ref.reshape(wide * HALO, LANES)
+            for d in range(HALO - 1 if place == 4 else HALO):
+                for j in range(nj):
+                    out[d * PER + place, j] = form(flat[pl.ds(row_of(d) + j * HALO, SUB, stride=nj * HALO), :])
 
     pl.when(lane == 0)(lambda: fill(0, 0, lambda d: d))
     pl.when(lane != 0)(lambda: fill(depth.shape[0] - wide, SUB - HALO, lambda d: HALO - 1 - d))
@@ -450,7 +443,7 @@
             pltpu.VMEM((3, wide, HALO, LANES), f32),
             pltpu.VMEM((wide, HALO, LANES), f32),
             pltpu.VMEM((wide, HALO, LANES), jnp.int32),
-            pltpu.SemaphoreType.DMA((3,)),
+            pltpu.SemaphoreType.DMA((5,)),
         ],
         compiler_params=params,
         name="pack",

time: 18.7 us -> 18.7 us (level)
  no operation moved by 1% of the time
where the time goes in v4:
time: 18.7 us; the launch traced here: 18.4 us
  Pallas kernels  12.7 us (68%)
  starting transfers between devices  4.53 us (24%)
  waiting for transfers between devices  1.06 us (6%)
    pallas_call x1, Pallas kernels, shards(): pl.pallas_call(functools.partial(middle_kernel, nj, bricks), out_shape=[j...  8.14 us
    ppermute x1, starting transfers between devices, shards(): near = lax.ppermute(packed, ('brick', 'cuts'), up + [(b, a) for a, b in up])  4.53 us
    pallas_call x2, Pallas kernels, edges(): pl.pallas_call(functools.partial(edge_kernel, nj, bricks, n, turned), out...  3.3 us
    pallas_call x1, Pallas kernels, shards(): pl.pallas_call(functools.partial(pack_kernel, nj), out_shape=jax.ShapeDty...  1.26 us
    ppermute x1, waiting for transfers between devices, shards(): near = lax.ppermute(packed, ('brick', 'cuts'), up + [(b, a) for a, b in up])  0.64 us
    ppermute x1, waiting for transfers between devices, shards(): other = lax.ppermute(near, 'cuts', [(0, 1), (1, 0)])  0.42 us
  transfers between devices with their start and end apart: 2, of which 2 were waited for; matrix products, arithmetic and copies ran while one was open for 0% of the time, Pallas kernels for 51%

profile of v4, /device:TPU:1, one launch (start us, length us, event | category | flops | bytes accessed | tf_op | source)
XLA Modules:
  0.0 18.4 jit_solution(3383166284186669006)
XLA Ops:
  0.0 0.0 copy-start
  0.0 0.0 copy-start.1
  0.0 0.0 copy-start.2
  0.0 1.3 %pack.1 = f32[19,5,8,128]{3,2,1,0:T(8,128)S(1)} custom-call(f32[3,160,8,128]{3,2,1,0:T(8,128)} %bitcast.27, f32[160,8,128]{2,1,0:T(8,128)} %bitcast.29, s32[160,8,128]{2,1,0:T(8,128)} %bitcast.31), custom_call_target="tpu_custom_call" | custom-call | tf_op jit(solution)/shard_map/pack/pallas_call | solution.py:437
  1.3 4.5 %collective-permute-start = (f32[19,5,8,128]{3,2,1,0:T(8,128)S(1)}, f32[19,5,8,128]{3,2,1,0:T(8,128)S(1)}, u32[]{:S(2)}, u32[]{:S(2)}) collective-permute-start(f32[19,5,8,128]{3,2,1,0:T(8,128)S(1)} %pack.1), channel_id=1, source_target_pairs={{1,2},{3,4},{5,6},{7,8},{9,10},{11,12},{13,14},{2,1},{4,3},{6,5},{... | collective-permute-start | bytes 1167368 | tf_op jit(solution)/shard_map/ppermute | solution.py:454
  5.8 0.0 copy-done
  5.8 0.0 copy-done.1
  5.8 0.0 copy-done.2
  5.8 8.1 %middle.1 = (f32[3,1280,128]{2,1,0:T(8,128)S(1)}, f32[32,3,5,8,128]{4,3,2,1,0:T(8,128)S(1)}, f32[32,4,5,8,128]{4,3,2,1,0:T(8,128)S(1)}, f32[32,3,5,8,128]{4,3,2,...) custom-call(f32[3,1280,128]{2,1,0:T(8,128)S(1)} %bitcast.28, ...), custom_call_target="tpu_custom_call" | custom-call | flops 49152000 | bytes 6553600 | tf_op jit(solution)/shard_map/middle/pallas_call | solution.py:456
  14.0 0.6 %collective-permute-done.near = f32[19,5,8,128]{3,2,1,0:T(8,128)S(1)} collective-permute-done((f32[19,5,8,128]{3,2,1,0:T(8,128)S(1)}, f32[19,5,8,128]{3,2,1,0:T(8,128)S(1)}, u32[]{:S(2)}, u32[]{:S(2)}) %collective-permute-start) | collective-permute-done | bytes 389152 | tf_op jit(solution)/shard_map/ppermute | solution.py:454
  14.6 0.0 collective-permute-start.1
  14.6 1.3 %edges.2 = (f32[3,160,8,128]{3,2,1,0:T(8,128)}, f32[3,320,128]{2,1,0:T(8,128)S(1)}) custom-call(f32[19,5,8,128]{3,2,1,0:T(8,128)S(1)} %collective-permute-done.near, f32[32,3,5,8,128]{4,3,2,1,0:T(8,128)S(1)} %get-tuple-element.44.ini, f32[32,4,5,8,128]{4,3,2,1,0:T(8,128)S(1)} %get-tuple-element.45.hw, f32[32,3,5,8,128]{4,3,2,1,0:T(8,128)S(1)} %get-tuple-element.46.s1, ...), custom_call_target="tpu_custom_call" | custom-call | flops 9830400 | bytes 655360 | tf_op jit(solution)/shard_map/edges/pallas_call | solution.py:483
  15.9 0.4 %collective-permute-done.1.near = f32[19,5,8,128]{3,2,1,0:T(8,128)S(1)} collective-permute-done((f32[19,5,8,128]{3,2,1,0:T(8,128)S(1)}, f32[19,5,8,128]{3,2,1,0:T(8,128)S(1)}, u32[]{:S(2)}, u32[]{:S(2)}) %collective-permute-start.1) | collective-permute-done | bytes 389152 | tf_op jit(solution)/shard_map/ppermute | solution.py:496
  16.4 2.0 %edges.3 = f32[3,160,8,128]{3,2,1,0:T(8,128)} custom-call(f32[19,5,8,128]{3,2,1,0:T(8,128)S(1)} %collective-permute-done.1.near, f32[32,3,5,8,128]{4,3,2,1,0:T(8,128)S(1)} %get-tuple-element.44.ini, f32[32,4,5,8,128]{4,3,2,1,0:T(8,128)S(1)} %get-tuple-element.45.hw, f32[32,3,5,8,128]{4,3,2,1,0:T(8,128)S(1)} %get-tuple-element.46.s1, ...), custom_call_target="tpu_custom_call", output_to_operand_aliasing={{}: (10, {})} | custom-call | flops 9830400 | bytes 655360 | tf_op jit(solution)/shard_map/edges/pallas_call | solution.py:483
Async XLA Ops:
  0.0 5.8 %copy-start = (f32[3,32,5120]{2,1,0:T(8,128)S(1)}, f32[3,32,5120]{2,1,0:T(8,128)}, u32[]{:S(2)}) copy-start(f32[3,32,5120]{2,1,0:T(8,128)} %param.3) | copy-start | bytes 5898244
  0.0 5.8 %copy-start.1 = (f32[32,5120]{1,0:T(8,128)S(1)}, f32[32,5120]{1,0:T(8,128)}, u32[]{:S(2)}) copy-start(f32[32,5120]{1,0:T(8,128)} %param.4) | copy-start | bytes 1966084
  0.0 5.8 %copy-start.2 = (s32[32,5120]{1,0:T(8,128)S(1)}, s32[32,5120]{1,0:T(8,128)}, u32[]{:S(2)}) copy-start(s32[32,5120]{1,0:T(8,128)} %param.5) | copy-start | bytes 1966084
  1.3 13.4 %collective-permute-start = (f32[19,5,8,128]{3,2,1,0:T(8,128)S(1)}, f32[19,5,8,128]{3,2,1,0:T(8,128)S(1)}, u32[]{:S(2)}, u32[]{:S(2)}) collective-permute-start(f32[19,5,8,128]{3,2,1,0:T(8,128)S(1)} %pack.1), channel_id=1, source_target_pairs={{1,2},{3,4},{5,6},{7,8},{9,10},{11,12},{13,14},{2,1},{4,3},{6,5},{... | collective-permute-start | bytes 1167368 | tf_op jit(solution)/shard_map/ppermute | solution.py:454
  14.6 1.7 %collective-permute-start.1 = (f32[19,5,8,128]{3,2,1,0:T(8,128)S(1)}, f32[19,5,8,128]{3,2,1,0:T(8,128)S(1)}, u32[]{:S(2)}, u32[]{:S(2)}) collective-permute-start(f32[19,5,8,128]{3,2,1,0:T(8,128)S(1)} %collective-permute-done.near), channel_id=1, source_target_pairs={{0,1},{1,0},{2,3},{3,2},{4,5},{5,4},{6,7},{7,6},{8,9},{9,8},{10,11... | collective-permute-start | bytes 1167368 | tf_op jit(solution)/shard_map/ppermute | solution.py:496
